TPU v7x, 32 devices: a whole 2x2x4 slice. The times are simulated.
32 devices in a mesh: section: 2 (over core), wide: 4 (over z), tensor: 4 (over y, x).
Axes of the slice: x: 2, y: 2, z: 4, core: 2. Of those that a mesh axis runs over, the one named last changes fastest.
Arguments:
- inputs: bfloat16 [2, 1, 4096, 768], P(None, None, 'wide'), may hold values from -6 to 6
- target: bfloat16 [2, 1, 4096, 768], P(None, None, 'wide'), may hold values from -1.1953125 to 1.1953125
- pad_mask: int32 [2, 1, 4096], replicated, may hold values from 0 to 1, as said below
- loss_mask: int32 [2, 1, 4096], replicated, may hold values from 0 to 1, as said below
- rand_blocks: int32 [2, 12, 64, 3], P('section', 'tensor'), may hold values from 0 to 63, as said below
- w_query: bfloat16 [2, 768, 768], P('section', None, 'tensor'), may hold values from -0.21875 to 0.21875
- b_query: bfloat16 [2, 768], P('section', 'tensor'), may hold values from -3 to 3
- w_key: bfloat16 [2, 768, 768], P('section', None, 'tensor'), may hold values from -0.21875 to 0.21875
- w_value: bfloat16 [2, 768, 768], P('section', None, 'tensor'), may hold values from -0.21875 to 0.21875
- b_value: bfloat16 [2, 768], P('section', 'tensor'), may hold values from -1.1953125 to 1.1953125
- w_out: bfloat16 [2, 768, 768], P('section', 'tensor'), may hold values from -0.875 to 0.875
- b_out: bfloat16 [2, 768], P('section'), may hold values from -3 to 3
- ln1_gain: bfloat16 [2, 768], P('section'), may hold values from 0.5 to 1.5
- ln1_bias: bfloat16 [2, 768], P('section'), may hold values from -1.796875 to 1.796875
- w_in: bfloat16 [2, 768, 3072], P('section', None, 'tensor'), may hold values from -0.21875 to 0.21875
- b_in: bfloat16 [2, 3072], P('section', 'tensor'), may hold values from -3 to 3
- w_ffn: bfloat16 [2, 3072, 768], P('section', 'tensor'), may hold values from -0.109375 to 0.109375
- b_ffn: bfloat16 [2, 768], P('section'), may hold values from -1.796875 to 1.796875
- ln2_gain: bfloat16 [2, 768], P('section'), may hold values from 0.5 to 1.5
- ln2_bias: bfloat16 [2, 768], P('section'), may hold values from -1.796875 to 1.796875
Outputs:
- layer_ends: bfloat16 [2, 2, 1, 4096, 768], P('section', None, None, 'wide')
- grad_w_query: float32 [2, 768, 768], P('section', None, 'tensor')
- grad_b_query: float32 [2, 768], P('section', 'tensor')
- grad_w_key: float32 [2, 768, 768], P('section', None, 'tensor')
- grad_w_value: float32 [2, 768, 768], P('section', None, 'tensor')
- grad_b_value: float32 [2, 768], P('section', 'tensor')
- grad_w_out: float32 [2, 768, 768], P('section', 'tensor')
- grad_b_out: float32 [2, 768], P('section')
- grad_ln1_gain: float32 [2, 768], P('section')
- grad_ln1_bias: float32 [2, 768], P('section')
- grad_w_in: float32 [2, 768, 3072], P('section', None, 'tensor')
- grad_b_in: float32 [2, 3072], P('section', 'tensor')
- grad_w_ffn: float32 [2, 3072, 768], P('section', 'tensor')
- grad_b_ffn: float32 [2, 768], P('section')
- grad_ln2_gain: float32 [2, 768], P('section')
- grad_ln2_bias: float32 [2, 768], P('section')
Inputs may be any that keep to these rules, and one draw needn't show every extreme that they name: `pad_mask`: real tokens form a prefix of each sequence of at least 2048 tokens; at least one sequence of the run has no padding. `loss_mask`: the first token of every sequence is marked. `rand_blocks`: for every layer, every index i of wide (block rows i * 16 to (i + 1) * 16 - 1) and every group of 3 consecutive heads, at most 36 of those rows' random blocks lie in the blocks of any one index of wide (blocks j * 16 to (j + 1) * 16 - 1), and exactly 36 in some.
All inputs are finite; a program needn't handle non-finite values.
Results may differ from a plain program's by a relative error of at most 0.023.
Values may be sent and summed in bfloat16 or wider, within the bound.
A program may use at most 384 MiB of HBM per device.

v0:
```python
from functools import partial

import jax
import jax.numpy as jnp
from jax import lax
from jax.sharding import PartitionSpec as P

HEAD_WIDTH = 64
BLK = 64


EPSILON = 1e-06
NEG_FILL = -1e30
HIGH_PRECISION = lax.Precision.HIGHEST


def swapped(value, axis, stride):
    mask = 2**stride
    pairs = [(source, source ^ mask) for source in range(lax.axis_size(axis))]
    return lax.ppermute(value, axis, pairs)


def joined(part, axis, combine):
    gathered = jax.tree.map(lambda a: lax.all_gather(a, axis), part)

    def take(source):
        return jax.tree.map(lambda a: lax.dynamic_index_in_dim(a, source, 0, False), gathered)

    return lax.fori_loop(
        1, lax.axis_size(axis), lambda source, state: combine(state, take(source)), take(0)
    )


def with_halo(block, sides, width):
    for axis, dim in sides:
        count = lax.axis_size(axis)
        forward = [(i, i + 1) for i in range(count - 1)]
        backward = [(target, source) for source, target in forward]
        low = lax.ppermute(
            lax.slice_in_dim(block, block.shape[dim] - width, None, axis=dim), axis, forward
        )
        high = lax.ppermute(lax.slice_in_dim(block, 0, width, axis=dim), axis, backward)
        block = jnp.concatenate([low, block, high], axis=dim)
    return block


def broadcast(block, axis, holder):
    block = jnp.where(lax.axis_index(axis) == holder, block, jnp.zeros_like(block))
    return lax.psum(block, axis)


def shortened(x):

    def short(part):
        return part.astype(jnp.bfloat16) if part.dtype == jnp.float32 else part

    return jax.tree.map(short, x)


def normalize(values, gain_vec, shift_vec):
    center = values - jnp.mean(values, axis=-1, keepdims=True)
    variance = jnp.mean(center * center, axis=-1, keepdims=True)
    return center * lax.rsqrt(variance + EPSILON) * gain_vec + shift_vec


def block_table(rand_rows, first_row, block_total):
    head_count, row_count, pick_count = rand_rows.shape
    row_ids = first_row + jnp.arange(row_count, dtype=jnp.int32)[:, None]
    fixed_ids = jnp.concatenate(
        [row_ids - 1, row_ids, row_ids + 1, jnp.zeros_like(row_ids), jnp.ones_like(row_ids)], axis=1
    )
    block_ids = jnp.concatenate(
        [jnp.broadcast_to(fixed_ids[None], (head_count, row_count, 5)), rand_rows], axis=2
    )
    slot_ids = jnp.arange(5 + pick_count)
    same_block = block_ids[..., :, None] == block_ids[..., None, :]
    earlier = slot_ids[:, None] > slot_ids[None, :]
    repeated = jnp.any(same_block & earlier, axis=-1)
    allowed = (block_ids >= 0) & (block_ids < block_total) & jnp.logical_not(repeated)
    return (jnp.clip(block_ids, 0, block_total - 1), allowed)


def tensor_total(partial_sum):
    shares = lax.psum_scatter(partial_sum, "tensor", scatter_dimension=2, tiled=True)
    return lax.all_gather(shares, "tensor", axis=2, tiled=True)


def section_trade(payload):
    return swapped(payload, "section", 0)


def merge_parts(first, second):
    peak = jnp.maximum(first[0], second[0])
    scale_first = jnp.exp(first[0] - peak)
    scale_second = jnp.exp(second[0] - peak)
    return (
        peak,
        first[1] * scale_first + second[1] * scale_second,
        first[2] * scale_first[..., None] + second[2] * scale_second[..., None],
    )


def random_plan(rand_local, wide_index, wide_count, blk_dev):
    head_count = rand_local.shape[0]
    pick_count = rand_local.shape[2]
    slot_count = head_count * blk_dev * pick_count
    capacity = -(-slot_count // wide_count)
    block_ids = rand_local.reshape(head_count, wide_count, blk_dev, pick_count).transpose(
        1, 0, 2, 3
    )
    owners = (block_ids // blk_dev).reshape(wide_count, slot_count)
    head_base = jnp.arange(head_count, dtype=jnp.int32)[None, :, None, None] * blk_dev
    local_row = (head_base + block_ids % blk_dev).reshape(wide_count, slot_count)
    slot_ids = jnp.arange(slot_count)
    same_owner = owners[:, :, None] == owners[:, None, :]
    earlier = slot_ids[:, None] > slot_ids[None, :]
    slot_rank = jnp.sum((same_owner & earlier[None]).astype(jnp.int32), axis=-1)
    place_ids = jnp.arange(capacity, dtype=jnp.int32)
    chosen = (
        (owners == wide_index)[:, None, :] & (slot_rank[:, None, :] == place_ids[None, :, None])
    ).astype(jnp.float32)
    row_hot = (
        local_row[:, :, None] == jnp.arange(head_count * blk_dev, dtype=jnp.int32)[None, None, :]
    ).astype(jnp.float32)
    send_pick = jnp.einsum("ics,isr->icr", chosen, row_hot, precision=HIGH_PRECISION)
    my_owner = lax.dynamic_index_in_dim(owners, wide_index, 0, keepdims=False)
    my_rank = lax.dynamic_index_in_dim(slot_rank, wide_index, 0, keepdims=False)
    recv_ids = jnp.arange(wide_count * capacity, dtype=jnp.int32)
    recv_pick = ((my_owner * capacity + my_rank)[:, None] == recv_ids[None, :]).astype(jnp.float32)
    return (send_pick, recv_pick)


def global_scores(glob_query, key_vals, key_ok_local):
    key_part = key_vals[..., :HEAD_WIDTH].astype(jnp.float32)
    score_matrix = jnp.einsum(
        "shqd,shkd->shqk", glob_query.astype(jnp.float32), key_part, precision=HIGH_PRECISION
    ) * HEAD_WIDTH ** (-0.5)
    usable = key_ok_local[:, None, None, :]
    return (jnp.where(usable, score_matrix, NEG_FILL), usable)


def global_rows(glob_query, key_vals, key_ok_local):
    value_part = key_vals[..., HEAD_WIDTH:].astype(jnp.float32)
    score_matrix, usable = global_scores(glob_query, key_vals, key_ok_local)
    peak = jnp.max(score_matrix, axis=-1)
    attention_weights = jnp.where(usable, jnp.exp(score_matrix - peak[..., None]), 0.0)
    parts = (
        peak,
        jnp.sum(attention_weights, axis=-1),
        jnp.einsum("shqk,shkd->shqd", attention_weights, value_part, precision=HIGH_PRECISION),
    )
    peak_all, total, accum = joined(parts, "wide", merge_parts)
    return (accum / total[..., None], peak_all + jnp.log(total))


def gather_context(queries, key_vals, key_ok_local, plan):
    seq_count, head_count, tok_local, pair_dim = key_vals.shape
    blk_dev = tok_local // BLK
    extended = with_halo(key_vals, (("wide", 2),), BLK)
    glob_both = broadcast(
        jnp.concatenate([queries[:, :, : 2 * BLK], key_vals[:, :, : 2 * BLK]], axis=-1), "wide", 0
    )
    local_blocks = key_vals.reshape(seq_count, head_count * blk_dev, BLK, pair_dim)
    outgoing = jnp.einsum(
        "icr,qrxy->qicxy",
        plan[0].astype(jnp.bfloat16),
        local_blocks,
        preferred_element_type=jnp.float32,
    ).astype(jnp.bfloat16)
    incoming = lax.all_to_all(outgoing, "wide", split_axis=1, concat_axis=1, tiled=True)
    flat_in = incoming.reshape(seq_count, -1, BLK, pair_dim)
    picked = jnp.einsum(
        "sj,qjxy->qsxy", plan[1].astype(jnp.bfloat16), flat_in, preferred_element_type=jnp.float32
    ).astype(jnp.bfloat16)
    rand_kv = picked.reshape(seq_count, head_count, blk_dev, -1, BLK, pair_dim)
    glob_out, glob_lse = global_rows(glob_both[..., :HEAD_WIDTH], key_vals, key_ok_local)
    return (extended, glob_both, rand_kv, glob_out, glob_lse)


def sparse_blocks(extended, glob_both, rand_kv):
    seq_count, head_count, ext_len, pair_dim = extended.shape
    blk_dev = ext_len // BLK - 2
    blocks = extended.reshape(seq_count, head_count, blk_dev + 2, BLK, pair_dim)
    window = jnp.stack([blocks[:, :, offset : offset + blk_dev] for offset in range(3)], axis=3)
    glob_kv = glob_both[..., HEAD_WIDTH:].reshape(seq_count, head_count, 1, 2, BLK, pair_dim)
    glob_kv = jnp.broadcast_to(glob_kv, (seq_count, head_count, blk_dev, 2, BLK, pair_dim))
    tiles = jnp.concatenate([window, glob_kv, rand_kv], axis=3)
    return tiles.reshape(seq_count, head_count, blk_dev, -1, pair_dim)


def sparse_scores(queries, key_block_tiles, usable):
    seq_count, head_count, tok_local, head_dim = queries.shape
    blk_dev = tok_local // BLK
    query_block_tiles = queries.reshape(seq_count, head_count, blk_dev, BLK, head_dim)
    score_matrix = jnp.einsum(
        "shbqd,shbnd->shbqn",
        query_block_tiles,
        key_block_tiles[..., :HEAD_WIDTH],
        preferred_element_type=jnp.float32,
    ) * HEAD_WIDTH ** (-0.5)
    usable_flat = usable.reshape(seq_count, head_count, blk_dev, 1, -1)
    return jnp.where(usable_flat, score_matrix, NEG_FILL)


def attend(queries, context, usable, glob_rows):
    extended, glob_both, rand_kv, glob_out, glob_lse = context
    seq_count, head_count, tok_local, head_dim = queries.shape
    key_block_tiles = sparse_blocks(extended, glob_both, rand_kv)
    score_matrix = sparse_scores(queries, key_block_tiles, usable)
    peak = jnp.max(score_matrix, axis=-1, keepdims=True)
    log_total = peak + jnp.log(jnp.sum(jnp.exp(score_matrix - peak), axis=-1, keepdims=True))
    attention_weights = jnp.exp(score_matrix - log_total).astype(jnp.bfloat16)
    sparse_output = jnp.einsum(
        "shbqn,shbnd->shbqd",
        attention_weights,
        key_block_tiles[..., HEAD_WIDTH:],
        preferred_element_type=jnp.float32,
    ).reshape(seq_count, head_count, tok_local, head_dim)
    glob_full = jnp.concatenate(
        [glob_out, jnp.zeros((seq_count, head_count, tok_local - 2 * BLK, head_dim), jnp.float32)],
        axis=2,
    )
    attended = jnp.where(glob_rows[None, None, :, None], glob_full, sparse_output)
    return (attended, log_total[..., 0])


def attend_back(
    queries, key_vals, context, usable, glob_rows, sparse_lse, d_out, plan, key_ok_local, wide_index
):
    extended, glob_both, rand_kv, glob_out, glob_lse = context
    seq_count, head_count, tok_local, head_dim = queries.shape
    pair_dim = key_vals.shape[3]
    blk_dev = tok_local // BLK
    logit_scale = HEAD_WIDTH ** (-0.5)
    key_block_tiles = sparse_blocks(extended, glob_both, rand_kv)
    score_matrix = sparse_scores(queries, key_block_tiles, usable)
    probs = jnp.exp(score_matrix - sparse_lse[..., None])
    probs_low = probs.astype(jnp.bfloat16)
    d_sparse = jnp.where(glob_rows[None, None, :, None], jnp.zeros_like(d_out), d_out)
    d_sparse = d_sparse.reshape(seq_count, head_count, blk_dev, BLK, head_dim)
    d_probs = jnp.einsum(
        "shbqd,shbnd->shbqn",
        d_sparse,
        key_block_tiles[..., HEAD_WIDTH:],
        preferred_element_type=jnp.float32,
    )
    d_scores = probs * (d_probs - jnp.sum(probs * d_probs, axis=-1, keepdims=True))
    d_low = d_scores.astype(jnp.bfloat16)
    query_block_tiles = queries.reshape(seq_count, head_count, blk_dev, BLK, head_dim)
    d_query = logit_scale * jnp.einsum(
        "shbqn,shbnd->shbqd",
        d_low,
        key_block_tiles[..., :HEAD_WIDTH],
        preferred_element_type=jnp.float32,
    )
    d_query = d_query.reshape(seq_count, head_count, tok_local, head_dim)
    d_keys = logit_scale * jnp.einsum(
        "shbqn,shbqd->shbnd", d_low, query_block_tiles, preferred_element_type=jnp.float32
    )
    d_vals = jnp.einsum(
        "shbqn,shbqd->shbnd", probs_low, d_sparse, preferred_element_type=jnp.float32
    )
    d_blocks = jnp.concatenate([d_keys, d_vals], axis=-1).reshape(
        seq_count, head_count, blk_dev, -1, BLK, pair_dim
    )
    window_part = d_blocks[:, :, :, :3]
    ext_grad = sum(
        (
            jnp.pad(
                window_part[:, :, :, offset], ((0, 0), (0, 0), (offset, 2 - offset), (0, 0), (0, 0))
            )
            for offset in range(3)
        )
    )
    local_grad = ext_grad[:, :, 1 : blk_dev + 1].reshape(seq_count, head_count, tok_local, pair_dim)
    rim_send = jnp.concatenate([ext_grad[:, :, 0], ext_grad[:, :, blk_dev + 1]], axis=2)
    rim_back = with_halo(rim_send.astype(jnp.bfloat16), (("wide", 2),), BLK).astype(rim_send.dtype)
    rest_pad = tok_local - BLK
    local_grad = local_grad + jnp.pad(rim_back[:, :, :BLK], ((0, 0), (0, 0), (0, rest_pad), (0, 0)))
    local_grad = local_grad + jnp.pad(
        rim_back[:, :, 3 * BLK :], ((0, 0), (0, 0), (rest_pad, 0), (0, 0))
    )
    glob_part = jnp.sum(d_blocks[:, :, :, 3:5], axis=2).reshape(
        seq_count, head_count, 2 * BLK, pair_dim
    )
    rand_part = d_blocks[:, :, :, 5:].reshape(seq_count, -1, BLK, pair_dim)
    glob_query = glob_both[..., :HEAD_WIDTH]
    glob_dout = broadcast(d_out[:, :, : 2 * BLK], "wide", 0).astype(jnp.float32)
    delta_glob = jnp.sum(glob_dout * glob_out, axis=-1)
    key_part = key_vals[..., :HEAD_WIDTH].astype(jnp.float32)
    value_part = key_vals[..., HEAD_WIDTH:].astype(jnp.float32)
    scores_glob, usable_glob = global_scores(glob_query, key_vals, key_ok_local)
    probs_glob = jnp.where(usable_glob, jnp.exp(scores_glob - glob_lse[..., None]), 0.0)
    dprob_glob = jnp.einsum("shqd,shkd->shqk", glob_dout, value_part, precision=HIGH_PRECISION)
    dscore_glob = probs_glob * (dprob_glob - delta_glob[..., None])
    dq_glob = logit_scale * jnp.einsum(
        "shqk,shkd->shqd", dscore_glob, key_part, precision=HIGH_PRECISION
    )
    dk_glob = logit_scale * jnp.einsum(
        "shqk,shqd->shkd", dscore_glob, glob_query.astype(jnp.float32), precision=HIGH_PRECISION
    )
    dv_glob = jnp.einsum("shqk,shqd->shkd", probs_glob, glob_dout, precision=HIGH_PRECISION)
    local_grad = local_grad + jnp.concatenate([dk_glob, dv_glob], axis=-1)
    dq_total, glob_total = lax.psum((dq_glob, glob_part), "wide")
    first_dev = wide_index == 0
    row_pad = ((0, 0), (0, 0), (0, tok_local - 2 * BLK), (0, 0))
    d_query = d_query + jnp.where(first_dev, jnp.pad(dq_total, row_pad), 0.0)
    local_grad = local_grad + jnp.where(first_dev, jnp.pad(glob_total, row_pad), 0.0)
    send_pick, recv_pick = plan
    wide_count, capacity = (send_pick.shape[0], send_pick.shape[1])
    outgoing = jnp.einsum("sj,qsxy->qjxy", recv_pick, rand_part, precision=HIGH_PRECISION)
    outgoing = outgoing.reshape(seq_count, wide_count, capacity, BLK, pair_dim)
    returned = lax.all_to_all(
        outgoing.astype(jnp.bfloat16), "wide", split_axis=1, concat_axis=1, tiled=True
    ).astype(outgoing.dtype)
    owned = jnp.einsum("icr,qicxy->qrxy", send_pick, returned, precision=HIGH_PRECISION)
    local_grad = local_grad + owned.reshape(seq_count, head_count, tok_local, pair_dim)
    return (d_query, local_grad)


def split_heads(flat, head_count):
    seq_count, tok_local, width_all = flat.shape
    return flat.reshape(seq_count, tok_local, head_count, -1).transpose(0, 2, 1, 3)


def join_heads(stacked):
    seq_count, head_count, tok_local, head_dim = stacked.shape
    return stacked.transpose(0, 2, 1, 3).reshape(seq_count, tok_local, head_count * head_dim)


def usable_blocks(key_ok, block_ids, allowed):
    seq_count = key_ok.shape[0]
    by_block = key_ok.reshape(seq_count, -1, BLK)
    return by_block[:, block_ids] & allowed[None, :, :, :, None]


def layer_forward(layer_in, key_ok, layer_params, plan, table_pair, wide_index):
    (
        w_query,
        b_query,
        w_key,
        w_value,
        b_value,
        w_out,
        b_out,
        gain_one,
        bias_one,
        w_in,
        b_in,
        w_ffn,
        b_ffn,
        gain_two,
        bias_two,
    ) = layer_params
    seq_count, tok_local, width_all = layer_in.shape
    head_count = w_query.shape[1] // HEAD_WIDTH
    key_ok_local = lax.dynamic_slice_in_dim(key_ok, wide_index * tok_local, tok_local, axis=1)
    usable = usable_blocks(key_ok, table_pair[0], table_pair[1])
    glob_rows = (wide_index == 0) & (jnp.arange(tok_local) < 2 * BLK)
    query_flat = jnp.einsum(
        "std,dc->stc", layer_in, w_query, preferred_element_type=jnp.float32
    ) + b_query.astype(jnp.float32)
    key_flat = jnp.einsum("std,dc->stc", layer_in, w_key, preferred_element_type=jnp.float32)
    value_flat = jnp.einsum(
        "std,dc->stc", layer_in, w_value, preferred_element_type=jnp.float32
    ) + b_value.astype(jnp.float32)
    queries = split_heads(query_flat.astype(jnp.bfloat16), head_count)
    key_vals = jnp.concatenate(
        [
            split_heads(key_flat.astype(jnp.bfloat16), head_count),
            split_heads(value_flat.astype(jnp.bfloat16), head_count),
        ],
        axis=-1,
    )
    context = gather_context(queries, key_vals, key_ok_local, plan)
    attended, sparse_lse = attend(queries, context, usable, glob_rows)
    attended_flat = join_heads(attended).astype(jnp.bfloat16)
    branch = tensor_total(
        jnp.einsum("stc,cd->std", attended_flat, w_out, preferred_element_type=jnp.float32)
    )
    resid_one = layer_in.astype(jnp.float32) + branch + b_out.astype(jnp.float32)
    mixed = normalize(resid_one, gain_one.astype(jnp.float32), bias_one.astype(jnp.float32)).astype(
        jnp.bfloat16
    )
    hidden = jnp.einsum(
        "std,df->stf", mixed, w_in, preferred_element_type=jnp.float32
    ) + b_in.astype(jnp.float32)
    active = jax.nn.gelu(hidden, approximate=True).astype(jnp.bfloat16)
    branch_two = tensor_total(
        jnp.einsum("stf,fd->std", active, w_ffn, preferred_element_type=jnp.float32)
    )
    resid_two = mixed.astype(jnp.float32) + branch_two + b_ffn.astype(jnp.float32)
    result = normalize(resid_two, gain_two.astype(jnp.float32), bias_two.astype(jnp.float32))
    memo = (
        layer_in,
        queries,
        key_vals,
        context,
        sparse_lse,
        attended_flat,
        resid_one,
        mixed,
        hidden,
        active,
        resid_two,
    )
    return (result, memo)


def layer_backward(memo, grad_out, key_ok, layer_params, plan, table_pair, wide_index):
    (
        w_query,
        b_query,
        w_key,
        w_value,
        b_value,
        w_out,
        b_out,
        gain_one,
        bias_one,
        w_in,
        b_in,
        w_ffn,
        b_ffn,
        gain_two,
        bias_two,
    ) = layer_params
    (
        layer_in,
        queries,
        key_vals,
        kept,
        sparse_lse,
        attended_flat,
        resid_one,
        mixed,
        hidden,
        active,
        resid_two,
    ) = memo
    seq_count, tok_local, width_all = layer_in.shape
    head_count = queries.shape[1]
    key_ok_local = lax.dynamic_slice_in_dim(key_ok, wide_index * tok_local, tok_local, axis=1)
    usable = usable_blocks(key_ok, table_pair[0], table_pair[1])
    glob_rows = (wide_index == 0) & (jnp.arange(tok_local) < 2 * BLK)
    norm_two, pull_two = jax.vjp(
        normalize, resid_two, gain_two.astype(jnp.float32), bias_two.astype(jnp.float32)
    )
    d_resid_two, d_gain_two, d_bias_two = pull_two(grad_out)
    d_b_ffn = jnp.sum(d_resid_two, axis=(0, 1))
    d_branch_two = d_resid_two.astype(jnp.bfloat16)
    d_w_ffn = jnp.einsum("stf,std->fd", active, d_branch_two, preferred_element_type=jnp.float32)
    d_active = jnp.einsum("std,fd->stf", d_branch_two, w_ffn, preferred_element_type=jnp.float32)
    gelu_value, gelu_pull = jax.vjp(partial(jax.nn.gelu, approximate=True), hidden)
    d_hidden = gelu_pull(d_active)[0].astype(jnp.bfloat16)
    d_b_in = jnp.sum(d_hidden.astype(jnp.float32), axis=(0, 1))
    d_w_in = jnp.einsum("std,stf->df", mixed, d_hidden, preferred_element_type=jnp.float32)
    d_mixed = d_resid_two + tensor_total(
        jnp.einsum("stf,df->std", d_hidden, w_in, preferred_element_type=jnp.float32)
    )
    norm_one, pull_one = jax.vjp(
        normalize, resid_one, gain_one.astype(jnp.float32), bias_one.astype(jnp.float32)
    )
    d_resid_one, d_gain_one, d_bias_one = pull_one(d_mixed)
    d_b_out = jnp.sum(d_resid_one, axis=(0, 1))
    d_branch = d_resid_one.astype(jnp.bfloat16)
    d_w_out = jnp.einsum("stc,std->cd", attended_flat, d_branch, preferred_element_type=jnp.float32)
    d_attended = jnp.einsum(
        "std,cd->stc", d_branch, w_out, preferred_element_type=jnp.float32
    ).astype(jnp.bfloat16)
    d_heads = split_heads(d_attended, head_count)
    d_query, d_key_vals = attend_back(
        queries,
        key_vals,
        kept,
        usable,
        glob_rows,
        sparse_lse,
        d_heads,
        plan,
        key_ok_local,
        wide_index,
    )
    d_query_flat = join_heads(d_query).astype(jnp.bfloat16)
    d_key_flat = join_heads(d_key_vals[..., :HEAD_WIDTH]).astype(jnp.bfloat16)
    d_value_flat = join_heads(d_key_vals[..., HEAD_WIDTH:]).astype(jnp.bfloat16)
    d_w_query = jnp.einsum(
        "std,stc->dc", layer_in, d_query_flat, preferred_element_type=jnp.float32
    )
    d_b_query = jnp.sum(d_query_flat.astype(jnp.float32), axis=(0, 1))
    d_w_key = jnp.einsum("std,stc->dc", layer_in, d_key_flat, preferred_element_type=jnp.float32)
    d_w_value = jnp.einsum(
        "std,stc->dc", layer_in, d_value_flat, preferred_element_type=jnp.float32
    )
    d_b_value = jnp.sum(d_value_flat.astype(jnp.float32), axis=(0, 1))
    back_part = (
        jnp.einsum("stc,dc->std", d_query_flat, w_query, preferred_element_type=jnp.float32)
        + jnp.einsum("stc,dc->std", d_key_flat, w_key, preferred_element_type=jnp.float32)
        + jnp.einsum("stc,dc->std", d_value_flat, w_value, preferred_element_type=jnp.float32)
    )
    d_input = d_resid_one + tensor_total(back_part)
    grads = (
        d_w_query,
        d_b_query,
        d_w_key,
        d_w_value,
        d_b_value,
        d_w_out,
        d_b_out,
        d_gain_one,
        d_bias_one,
        d_w_in,
        d_b_in,
        d_w_ffn,
        d_b_ffn,
        d_gain_two,
        d_bias_two,
    )
    return (d_input, grads)


def pick_section(upper_part, lower_part, is_last):
    return jax.tree.map(partial(jnp.where, is_last), upper_part, lower_part)


def body(
    inputs,
    target,
    pad_mask,
    loss_mask,
    rand_blocks,
    w_query,
    b_query,
    w_key,
    w_value,
    b_value,
    w_out,
    b_out,
    ln1_gain,
    ln1_bias,
    w_in,
    b_in,
    w_ffn,
    b_ffn,
    ln2_gain,
    ln2_bias,
):
    section_id = lax.axis_index("section")
    wide_index = lax.axis_index("wide")
    wide_count = lax.axis_size("wide")
    layer_params = tuple(
        (
            weight[0]
            for weight in (
                w_query,
                b_query,
                w_key,
                w_value,
                b_value,
                w_out,
                b_out,
                ln1_gain,
                ln1_bias,
                w_in,
                b_in,
                w_ffn,
                b_ffn,
                ln2_gain,
                ln2_bias,
            )
        )
    )
    micro_count, seq_count, tok_local, width_all = inputs.shape
    sequence_length = pad_mask.shape[2]
    blk_dev = tok_local // BLK
    block_total = sequence_length // BLK
    rand_local = rand_blocks[0]
    plan = random_plan(rand_local, wide_index, wide_count, blk_dev)
    rand_rows = lax.dynamic_slice_in_dim(rand_local, wide_index * blk_dev, blk_dev, axis=1)
    table_pair = block_table(rand_rows, wide_index * blk_dev, block_total)
    key_ok_all = pad_mask > 0
    weight_all = (loss_mask * pad_mask).astype(jnp.float32)
    factor = seq_count * sequence_length / jnp.sum(weight_all, axis=(1, 2))
    weight_local = lax.dynamic_slice_in_dim(weight_all, wide_index * tok_local, tok_local, axis=2)
    is_last = section_id == 1
    received = jnp.zeros((seq_count, tok_local, width_all), jnp.bfloat16)
    saved = []
    layer_outputs = []
    for time_step in range(micro_count + 1):
        micro_index = jnp.clip(time_step - section_id, 0, micro_count - 1)
        fresh = inputs[min(time_step, micro_count - 1)]
        layer_in = jnp.where(section_id == 0, fresh, received)
        key_ok = lax.dynamic_index_in_dim(key_ok_all, micro_index, 0, keepdims=False)
        result, memo = layer_forward(layer_in, key_ok, layer_params, plan, table_pair, wide_index)
        saved.append(memo)
        sent = result.astype(jnp.bfloat16)
        layer_outputs.append(sent)
        if time_step < micro_count:
            received = section_trade(sent)
    totals = tuple((jnp.zeros(param.shape, jnp.float32) for param in layer_params))
    back_recv = jnp.zeros((seq_count, tok_local, width_all), jnp.bfloat16)
    input_grads = []
    for time_step in range(micro_count + 1):
        micro_index = jnp.clip(time_step - 1 + section_id, 0, micro_count - 1)
        memo = pick_section(
            saved[min(time_step + 1, micro_count)], saved[max(time_step - 1, 0)], is_last
        )
        last_micro = min(time_step, micro_count - 1)
        loss_grad = (
            target[last_micro].astype(jnp.float32)
            * (weight_local[last_micro] * factor[last_micro])[..., None]
        )
        grad_in = jnp.where(is_last, loss_grad, back_recv.astype(jnp.float32))
        key_ok = lax.dynamic_index_in_dim(key_ok_all, micro_index, 0, keepdims=False)
        d_input, grads = layer_backward(
            memo, grad_in, key_ok, layer_params, plan, table_pair, wide_index
        )
        valid = jnp.where(is_last, time_step < micro_count, time_step >= 1)
        totals = tuple((total + jnp.where(valid, grad, 0.0) for total, grad in zip(totals, grads)))
        sent = d_input.astype(jnp.bfloat16)
        input_grads.append(sent)
        if time_step < micro_count:
            back_recv = section_trade(sent)
    summed = jax.tree.map(
        lambda part: part.astype(jnp.float32), lax.psum(shortened(totals), "wide")
    )
    outputs_stack = jnp.stack(layer_outputs[1:])
    grads_stack = jnp.stack(input_grads[1:])
    layer_ends = jnp.where(is_last, outputs_stack, grads_stack)[None]
    return (
        layer_ends,
        summed[0][None],
        summed[1][None],
        summed[2][None],
        summed[3][None],
        summed[4][None],
        summed[5][None],
        summed[6][None],
        summed[7][None],
        summed[8][None],
        summed[9][None],
        summed[10][None],
        summed[11][None],
        summed[12][None],
        summed[13][None],
        summed[14][None],
    )


def solution(mesh):
    return jax.shard_map(
        body,
        mesh=mesh,
        in_specs=(
            P(None, None, "wide", None),
            P(None, None, "wide", None),
            P(),
            P(),
            P("section", "tensor", None, None),
            P("section", None, "tensor"),
            P("section", "tensor"),
            P("section", None, "tensor"),
            P("section", None, "tensor"),
            P("section", "tensor"),
            P("section", "tensor", None),
            P("section", None),
            P("section", None),
            P("section", None),
            P("section", None, "tensor"),
            P("section", "tensor"),
            P("section", "tensor", None),
            P("section", None),
            P("section", None),
            P("section", None),
        ),
        out_specs=(
            P("section", None, None, "wide", None),
            P("section", None, "tensor"),
            P("section", "tensor"),
            P("section", None, "tensor"),
            P("section", None, "tensor"),
            P("section", "tensor"),
            P("section", "tensor", None),
            P("section", None),
            P("section", None),
            P("section", None),
            P("section", None, "tensor"),
            P("section", "tensor"),
            P("section", "tensor", None),
            P("section", None),
            P("section", None),
            P("section", None),
        ),
        check_vma=False,
    )
```

profile of v0, /device:TPU:0, one launch (start us, length us, event | category | flops | bytes accessed | tf_op | source)
XLA Modules:
  0.0 3371.5 jit_solution(12071089696481920367)
XLA Ops:
  58.2 40.8 %all-gather.2 = f32[12,128,64]{1,2,0:T(8,128)S(1)} all-gather(f32[3,128,64]{1,2,0:T(8,128)S(1)} %fusion.269), channel_id=4, replica_groups=mesh['section'=2,'wide'=4,'tensor'=4] {'wide'}, dimensions={0}, use_global_device_ids=true | all-gather | bytes 491520 | tf_op jit(solution)/shard_map/all_gather | solution.py:24
  100.9 12.1 all-gather.10
  113.1 11.9 all-gather.9
  166.8 84.0 %all-reduce.67.cloned.1.call-done = f32[1,1024,768]{1,0,2:T(1,128)} async-done(((f32[1,1024,768]{1,0,2:T(1,128)}), f32[1,1024,768]{1,0,2:T(1,128)}) %all-reduce.67.cloned.1.call-update) | async-done | bytes 3145744
  265.0 32.6 all-gather.28.cloned.1.call-done
  326.1 87.3 %all-reduce.69.cloned.1.call-done = f32[1,1024,768]{1,0,2:T(1,128)} async-done(((f32[1,1024,768]{1,0,2:T(1,128)}), f32[1,1024,768]{1,0,2:T(1,128)}) %all-reduce.69.cloned.1.call-update) | async-done | bytes 3145744
  417.4 42.7 %all-gather.30.cloned.1.call-done = f32[1,1024,768]{1,0,2:T(1,128)} async-done(((f32[1,1024,192]{1,0,2:T(1,128)}), f32[1,1024,768]{1,0,2:T(1,128)}) %all-gather.30.cloned.1.call-update) | async-done | bytes 3145744 | tf_op jit(solution)/shard_map/all_gather | solution.py:85
  535.0 38.8 %all-gather.5 = f32[12,128,64]{1,2,0:T(8,128)S(1)} all-gather(f32[3,128,64]{1,2,0:T(8,128)S(1)} %fusion.271), channel_id=7, replica_groups=mesh['section'=2,'wide'=4,'tensor'=4] {'wide'}, dimensions={0}, use_global_device_ids=true | all-gather | bytes 491520 | tf_op jit(solution)/shard_map/all_gather | solution.py:24
  578.7 11.9 all-gather.12
  591.1 12.3 all-gather.11
  604.0 22.9 while.58
  673.9 84.9 %all-reduce.71.cloned.1.call-done = f32[1,1024,768]{1,0,2:T(1,128)} async-done(((f32[1,1024,768]{1,0,2:T(1,128)}), f32[1,1024,768]{1,0,2:T(1,128)}) %all-reduce.71.cloned.1.call-update) | async-done | bytes 3145744
  761.6 43.9 %all-gather.32.cloned.1.call-done = f32[1,1024,768]{1,0,2:T(1,128)} async-done(((f32[1,1024,192]{1,0,2:T(1,128)}), f32[1,1024,768]{1,0,2:T(1,128)}) %all-gather.32.cloned.1.call-update) | async-done | bytes 3145744 | tf_op jit(solution)/shard_map/all_gather | solution.py:85
  843.6 87.3 %all-reduce.73.cloned.1.call-done = f32[1,1024,768]{1,0,2:T(1,128)} async-done(((f32[1,1024,768]{1,0,2:T(1,128)}), f32[1,1024,768]{1,0,2:T(1,128)}) %all-reduce.73.cloned.1.call-update) | async-done | bytes 3145744
  936.9 40.7 %all-gather.34.cloned.1.call-done = f32[1,1024,768]{1,0,2:T(1,128)} async-done(((f32[1,1024,192]{1,0,2:T(1,128)}), f32[1,1024,768]{1,0,2:T(1,128)}) %all-gather.34.cloned.1.call-update) | async-done | bytes 3145744 | tf_op jit(solution)/shard_map/all_gather | solution.py:85
  1080.7 39.9 %all-gather.8 = f32[12,128,64]{1,2,0:T(8,128)S(1)} all-gather(f32[3,128,64]{1,2,0:T(8,128)S(1)} %fusion.273), channel_id=10, replica_groups=mesh['section'=2,'wide'=4,'tensor'=4] {'wide'}, dimensions={0}, use_global_device_ids=true | all-gather | bytes 491520 | tf_op jit(solution)/shard_map/all_gather | solution.py:24
  1123.7 12.0 all-gather.14
  1136.3 11.9 all-gather.13
  1148.8 23.0 while.59
  1229.1 136.5 %all-reduce.85.cloned.1.call-done = (f32[1,1024,768]{1,0,2:T(1,128)}, f32[1,1024,768]{1,0,2:T(1,128)}) async-done(((f32[1,1024,768]{1,0,2:T(1,128)}, f32[1,1024,768]{1,0,2:T(1,128)}), (f32[1,1024,768]{1,0,2:T(1,128)}, f32[1,1024,768]{1,0,2:T(1,128)})) %all-reduce.85.cloned.1.call-update) | async-done | bytes 6291472
  1387.4 24.9 all-gather.40.cloned.1.call-done
  1427.8 30.9 all-gather.36.cloned.1.call-done
  1538.0 11.7 copy_dynamic-update-slice_fusion.5
  1549.8 11.7 copy_dynamic-update-slice_fusion.4
  1565.9 11.9 slice.566
  1583.9 21.0 psum.192
  1682.0 34.4 %all-reduce.91.cloned.1.call-done = (f32[1,3,128,64]{2,3,1,0:T(8,128)}, f32[1,3,128,128]{2,3,1,0:T(8,128)}) async-done(((f32[1,3,128,64]{2,3,1,0:T(8,128)}, f32[1,3,128,128]{2,3,1,0:T(8,128)}), (f32[1,3,128,64]{2,3,1,0:T(8,128)}, f32[1,3,128,128]{2,3,1,0:T(8,128)})) %all-reduce.91.cloned.1.call-update) | async-done | bytes 294928 | tf_op jit(solution)/shard_map/psum | solution.py:304
  1743.8 138.7 %all-reduce.83.cloned.1.call-done = (f32[1,1024,768]{1,0,2:T(1,128)}, f32[1,1024,768]{1,0,2:T(1,128)}) async-done(((f32[1,1024,768]{1,0,2:T(1,128)}, f32[1,1024,768]{1,0,2:T(1,128)}), (f32[1,1024,768]{1,0,2:T(1,128)}, f32[1,1024,768]{1,0,2:T(1,128)})) %all-reduce.83.cloned.1.call-update) | async-done | bytes 6291472
  1888.1 41.0 %all-gather.38.cloned.1.call-done = f32[1,1024,768]{1,0,2:T(1,128)} async-done(((f32[1,1024,192]{1,0,2:T(1,128)}), f32[1,1024,768]{1,0,2:T(1,128)}) %all-gather.38.cloned.1.call-update) | async-done | bytes 3145744 | tf_op jit(solution)/shard_map/all_gather | solution.py:85
  1946.9 28.7 all-gather.42.cloned.1.call-done
  2017.4 87.3 %all-reduce.75.cloned.1.call-done = f32[1,1024,768]{1,0,2:T(1,128)} async-done(((f32[1,1024,768]{1,0,2:T(1,128)}), f32[1,1024,768]{1,0,2:T(1,128)}) %all-reduce.75.cloned.1.call-update) | async-done | bytes 3145744
  2118.9 32.5 all-gather.44.cloned.1.call-done
  2219.1 11.7 copy_dynamic-update-slice_fusion.3
  2230.8 11.7 copy_dynamic-update-slice_fusion.2
  2290.6 56.7 %psum.195 = bf16[1,3,128,64]{2,3,1,0:T(8,128)(2,1)} all-reduce(bf16[1,3,128,64]{2,3,1,0:T(8,128)(2,1)} %slice_select_fusion.2), channel_id=1, replica_groups=mesh['section'=2,'wide'=4,'tensor'=4] {'wide'}, use_global_device_ids=true, to_apply=%region_68.69 | all-reduce | flops 24576 | bytes 98304 | tf_op jit(solution)/shard_map/psum | solution.py:49
  2387.3 33.2 all-reduce.89.cloned.1.call-done
  2447.9 87.1 %all-reduce.77.cloned.1.call-done = f32[1,1024,768]{1,0,2:T(1,128)} async-done(((f32[1,1024,768]{1,0,2:T(1,128)}), f32[1,1024,768]{1,0,2:T(1,128)}) %all-reduce.77.cloned.1.call-update) | async-done | bytes 3145744
  2537.6 44.1 %all-gather.46.cloned.1.call-done = f32[1,1024,768]{1,0,2:T(1,128)} async-done(((f32[1,1024,192]{1,0,2:T(1,128)}), f32[1,1024,768]{1,0,2:T(1,128)}) %all-gather.46.cloned.1.call-update) | async-done | bytes 3145744 | tf_op jit(solution)/shard_map/all_gather | solution.py:85
  2633.1 75.2 %all-reduce.79.cloned.1.call-done = f32[1,1024,768]{1,0,2:T(1,128)} async-done(((f32[1,1024,768]{1,0,2:T(1,128)}), f32[1,1024,768]{1,0,2:T(1,128)}) %all-reduce.79.cloned.1.call-update) | async-done | bytes 3145744
  2737.3 17.9 all-gather.48.cloned.1.call-done
  2822.7 11.6 copy_dynamic-update-slice_fusion.1
  2834.3 11.5 copy_dynamic-update-slice_fusion
  2894.0 56.8 %psum.198 = bf16[1,3,128,64]{2,3,1,0:T(8,128)(2,1)} all-reduce(bf16[1,3,128,64]{2,3,1,0:T(8,128)(2,1)} %slice_select_fusion.1), channel_id=1, replica_groups=mesh['section'=2,'wide'=4,'tensor'=4] {'wide'}, use_global_device_ids=true, to_apply=%region_84.85 | all-reduce | flops 24576 | bytes 98304 | tf_op jit(solution)/shard_map/psum | solution.py:49
  2991.3 33.0 all-reduce.87.cloned.1.call-done
  3069.7 69.1 %all-reduce.81.cloned.1.call-done = f32[1,1024,768]{1,0,2:T(1,128)} async-done(((f32[1,1024,768]{1,0,2:T(1,128)}), f32[1,1024,768]{1,0,2:T(1,128)}) %all-reduce.81.cloned.1.call-update) | async-done | bytes 3145744
  3149.8 128.9 %all-reduce.93.cloned.1.call-done = (bf16[1,768,192]{1,2,0:T(8,128)(2,1)}, bf16[1,768,192]{1,2,0:T(8,128)(2,1)}, bf16[1,768,192]{1,2,0:T(8,128)(2,1)}, bf16[1,19...) async-done(((bf16[1,768,192]{1,2,0:T(8,128)(2,1)}, bf16[1,768,192]{1,2,0:T(8,128)(2,1)}, bf16[1,768,192]{1,2,0:T(8,128)(2,1)}, ...) | async-done | bytes 3538960 | tf_op jit(solution)/shard_map/psum | solution.py:625
  3286.6 36.8 %all-gather.50.cloned.1.call-done = f32[1,1024,768]{1,0,2:T(1,128)} async-done(((f32[1,1024,192]{1,0,2:T(1,128)}), f32[1,1024,768]{1,0,2:T(1,128)}) %all-gather.50.cloned.1.call-update) | async-done | bytes 3145744 | tf_op jit(solution)/shard_map/all_gather | solution.py:85
  3336.6 18.9 all-reduce.41
  (1357 shorter events, 1343.2 us)
Async XLA Ops:
  7.2 48.4 %all-reduce.61.cloned.1.call-start = ((), (), s32[]{:S(2)}) async-start(), calls=%async_computation.6 | async-start | bytes 294912 | tf_op jit(solution)/shard_map/psum | solution.py:49
  14.5 33.0 collective-permute-start
  20.0 27.4 collective-permute-start.1
  28.2 100.7 %all-to-all-start = ((bf16[1,4,36,64,128]{4,3,2,0,1:T(8,128)(2,1)}), bf16[1,4,36,64,128]{4,3,2,0,1:T(8,128)(2,1)}, u32[]{:S(2)}, u32[]{:S(2)}) async-start(bf16[1,4,36,64,128]{4,3,2,0,1:T(8,128)(2,1)} %copy.584), calls=%async_computation | async-start | bytes 4718592 | tf_op jit(solution)/shard_map/all_to_all | solution.py:170
  34.2 216.6 %all-reduce.67.cloned.1.call-start = ((), (), s32[]{:S(2)}) async-start(), calls=%async_computation.21 | async-start | bytes 6291456
  165.0 132.6 %all-gather.28.cloned.1.call-start = ((), (), s32[]{:S(2)}) async-start(), calls=%async_computation.7 | async-start | bytes 3932160 | tf_op jit(solution)/shard_map/all_gather | solution.py:85
  253.4 160.0 %all-reduce.69.cloned.1.call-start = ((), (), s32[]{:S(2)}) async-start(), calls=%async_computation.22 | async-start | bytes 6291456
  326.0 134.1 %all-gather.30.cloned.1.call-start = ((), (), s32[]{:S(2)}) async-start(), calls=%async_computation.8 | async-start | bytes 3932160 | tf_op jit(solution)/shard_map/all_gather | solution.py:85
  416.0 114.1 %all-reduce.63.cloned.1.call-start = ((), (), s32[]{:S(2)}) async-start(), calls=%async_computation.9 | async-start | bytes 294912 | tf_op jit(solution)/shard_map/psum | solution.py:49
  490.8 17.7 collective-permute-start.3
  494.8 13.7 collective-permute-start.4
  502.7 133.2 %all-to-all-start.1 = ((bf16[1,4,36,64,128]{4,3,2,0,1:T(8,128)(2,1)}), bf16[1,4,36,64,128]{4,3,2,0,1:T(8,128)(2,1)}, u32[]{:S(2)}, u32[]{:S(2)}) async-start(bf16[1,4,36,64,128]{4,3,2,0,1:T(8,128)(2,1)} %copy.608), calls=%async_computation.1 | async-start | bytes 4718592 | tf_op jit(solution)/shard_map/all_to_all | solution.py:170
  508.5 250.3 %all-reduce.71.cloned.1.call-start = ((), (), s32[]{:S(2)}) async-start(), calls=%async_computation.23 | async-start | bytes 6291456
  673.8 131.7 %all-gather.32.cloned.1.call-start = ((), (), s32[]{:S(2)}) async-start(), calls=%async_computation.10 | async-start | bytes 3932160 | tf_op jit(solution)/shard_map/all_gather | solution.py:85
  761.3 169.5 %all-reduce.73.cloned.1.call-start = ((), (), s32[]{:S(2)}) async-start(), calls=%async_computation.24 | async-start | bytes 6291456
  843.5 134.1 %all-gather.34.cloned.1.call-start = ((), (), s32[]{:S(2)}) async-start(), calls=%async_computation.11 | async-start | bytes 3932160 | tf_op jit(solution)/shard_map/all_gather | solution.py:85
  933.5 143.4 %all-reduce.65.cloned.1.call-start = ((), (), s32[]{:S(2)}) async-start(), calls=%async_computation.12 | async-start | bytes 294912 | tf_op jit(solution)/shard_map/psum | solution.py:49
  1005.3 17.3 collective-permute-start.5
  1036.7 17.7 collective-permute-start.6
  1040.8 13.7 collective-permute-start.7
  1048.7 148.7 %all-to-all-start.2 = ((bf16[1,4,36,64,128]{4,3,2,0,1:T(8,128)(2,1)}), bf16[1,4,36,64,128]{4,3,2,0,1:T(8,128)(2,1)}, u32[]{:S(2)}, u32[]{:S(2)}) async-start(bf16[1,4,36,64,128]{4,3,2,0,1:T(8,128)(2,1)} %copy.632), calls=%async_computation.2 | async-start | bytes 4718592 | tf_op jit(solution)/shard_map/all_to_all | solution.py:170
  1054.5 311.1 %all-reduce.85.cloned.1.call-start = ((), (), s32[]{:S(2)}) async-start(), calls=%async_computation.30 | async-start | bytes 12582912
  1229.0 183.3 %all-gather.40.cloned.1.call-start = ((), (), s32[]{:S(2)}) async-start(), calls=%async_computation.15 | async-start | bytes 3932160 | tf_op jit(solution)/shard_map/all_gather | solution.py:85
  1368.2 90.6 %all-gather.36.cloned.1.call-start = ((), (), s32[]{:S(2)}) async-start(), calls=%async_computation.13 | async-start | bytes 3932160 | tf_op jit(solution)/shard_map/all_gather | solution.py:85
  1578.6 101.5 %collective-permute-start.8 = (bf16[1,3,64,128]{2,3,1,0:T(8,128)(2,1)}, bf16[1,3,64,128]{2,3,1,0:T(8,128)(2,1)}, u32[]{:S(2)}, u32[]{:S(2)}) collective-permute-start(bf16[1,3,64,128]{2,3,1,0:T(8,128)(2,1)} %bitcast.213), channel_id=1, source_target_pairs={{0,4},{4,8},{8,12},{1,5},{5,9},{9,13},{2,6},{6,10},{10,14},{3,7},{... | collective-permute-start | bytes 147464 | tf_op jit(solution)/shard_map/ppermute | solution.py:39
  1582.6 97.5 %collective-permute-start.9 = (bf16[1,3,64,128]{2,3,1,0:T(8,128)(2,1)}, bf16[1,3,64,128]{2,3,1,0:T(8,128)(2,1)}, u32[]{:S(2)}, u32[]{:S(2)}) collective-permute-start(bf16[1,3,64,128]{2,3,1,0:T(8,128)(2,1)} %bitcast.217), channel_id=1, source_target_pairs={{4,0},{8,4},{12,8},{5,1},{9,5},{13,9},{6,2},{10,6},{14,10},{7,3},{... | collective-permute-start | bytes 147464 | tf_op jit(solution)/shard_map/ppermute | solution.py:42
  1624.5 97.8 %all-to-all-start.3 = ((bf16[1,4,36,64,128]{4,3,2,0,1:T(8,128)(2,1)}), bf16[1,4,36,64,128]{4,3,2,0,1:T(8,128)(2,1)S(1)}, u32[]{:S(2)}, u32[]{:S(2)}) async-start(bf16[1,4,36,64,128]{4,3,2,0,1:T(8,128)(2,1)} %bitcast.1217), calls=%async_computation.3 | async-start | bytes 4718592 | tf_op jit(solution)/shard_map/all_to_all | solution.py:313
  1628.1 88.3 %all-reduce.91.cloned.1.call-start = ((), (), s32[]{:S(2)}) async-start(), calls=%async_computation.33 | async-start | bytes 589824 | tf_op jit(solution)/shard_map/psum | solution.py:304
  1679.8 202.6 %all-reduce.83.cloned.1.call-start = ((), (), s32[]{:S(2)}) async-start(), calls=%async_computation.29 | async-start | bytes 12582912
  1743.7 185.4 %all-gather.38.cloned.1.call-start = ((), (), s32[]{:S(2)}) async-start(), calls=%async_computation.14 | async-start | bytes 3932160 | tf_op jit(solution)/shard_map/all_gather | solution.py:85
  1885.0 90.6 %all-gather.42.cloned.1.call-start = ((), (), s32[]{:S(2)}) async-start(), calls=%async_computation.16 | async-start | bytes 3932160 | tf_op jit(solution)/shard_map/all_gather | solution.py:85
  1887.7 217.0 %all-reduce.75.cloned.1.call-start = ((), (), s32[]{:S(2)}) async-start(), calls=%async_computation.25 | async-start | bytes 6291456
  2017.3 134.1 %all-gather.44.cloned.1.call-start = ((), (), s32[]{:S(2)}) async-start(), calls=%async_computation.17 | async-start | bytes 3932160 | tf_op jit(solution)/shard_map/all_gather | solution.py:85
  2277.0 149.4 %all-to-all-start.4 = ((bf16[1,4,36,64,128]{4,3,2,0,1:T(8,128)(2,1)}), bf16[1,4,36,64,128]{4,3,2,0,1:T(8,128)(2,1)S(1)}, u32[]{:S(2)}, u32[]{:S(2)}) async-start(bf16[1,4,36,64,128]{4,3,2,0,1:T(8,128)(2,1)} %bitcast.1216), calls=%async_computation.4 | async-start | bytes 4718592 | tf_op jit(solution)/shard_map/all_to_all | solution.py:313
  2281.5 138.9 %all-reduce.89.cloned.1.call-start = ((), (), s32[]{:S(2)}) async-start(), calls=%async_computation.32 | async-start | bytes 589824 | tf_op jit(solution)/shard_map/psum | solution.py:304
  2283.3 102.0 %collective-permute-start.11 = (bf16[1,3,64,128]{2,3,1,0:T(8,128)(2,1)}, bf16[1,3,64,128]{2,3,1,0:T(8,128)(2,1)}, u32[]{:S(2)}, u32[]{:S(2)}) collective-permute-start(bf16[1,3,64,128]{2,3,1,0:T(8,128)(2,1)} %bitcast.268), channel_id=1, source_target_pairs={{0,4},{4,8},{8,12},{1,5},{5,9},{9,13},{2,6},{6,10},{10,14},{3,7},{... | collective-permute-start | bytes 147464 | tf_op jit(solution)/shard_map/ppermute | solution.py:39
  2287.9 97.4 %collective-permute-start.12 = (bf16[1,3,64,128]{2,3,1,0:T(8,128)(2,1)}, bf16[1,3,64,128]{2,3,1,0:T(8,128)(2,1)}, u32[]{:S(2)}, u32[]{:S(2)}) collective-permute-start(bf16[1,3,64,128]{2,3,1,0:T(8,128)(2,1)} %bitcast.272), channel_id=1, source_target_pairs={{4,0},{8,4},{12,8},{5,1},{9,5},{13,9},{6,2},{10,6},{14,10},{7,3},{... | collective-permute-start | bytes 147464 | tf_op jit(solution)/shard_map/ppermute | solution.py:42
  2385.1 149.9 %all-reduce.77.cloned.1.call-start = ((), (), s32[]{:S(2)}) async-start(), calls=%async_computation.26 | async-start | bytes 6291456
  2447.9 133.8 %all-gather.46.cloned.1.call-start = ((), (), s32[]{:S(2)}) async-start(), calls=%async_computation.18 | async-start | bytes 3932160 | tf_op jit(solution)/shard_map/all_gather | solution.py:85
  2537.6 170.7 %all-reduce.79.cloned.1.call-start = ((), (), s32[]{:S(2)}) async-start(), calls=%async_computation.27 | async-start | bytes 6291456
  2621.0 134.2 %all-gather.48.cloned.1.call-start = ((), (), s32[]{:S(2)}) async-start(), calls=%async_computation.19 | async-start | bytes 3932160 | tf_op jit(solution)/shard_map/all_gather | solution.py:85
  2880.3 149.9 %all-to-all-start.5 = ((bf16[1,4,36,64,128]{4,3,2,0,1:T(8,128)(2,1)}), bf16[1,4,36,64,128]{4,3,2,0,1:T(8,128)(2,1)S(1)}, u32[]{:S(2)}, u32[]{:S(2)}) async-start(bf16[1,4,36,64,128]{4,3,2,0,1:T(8,128)(2,1)} %bitcast.1215), calls=%async_computation.5 | async-start | bytes 4718592 | tf_op jit(solution)/shard_map/all_to_all | solution.py:313
  2884.9 139.4 %all-reduce.87.cloned.1.call-start = ((), (), s32[]{:S(2)}) async-start(), calls=%async_computation.31 | async-start | bytes 589824 | tf_op jit(solution)/shard_map/psum | solution.py:304
  2886.7 102.6 %collective-permute-start.14 = (bf16[1,3,64,128]{2,3,1,0:T(8,128)(2,1)}, bf16[1,3,64,128]{2,3,1,0:T(8,128)(2,1)}, u32[]{:S(2)}, u32[]{:S(2)}) collective-permute-start(bf16[1,3,64,128]{2,3,1,0:T(8,128)(2,1)} %bitcast.322), channel_id=1, source_target_pairs={{0,4},{4,8},{8,12},{1,5},{5,9},{9,13},{2,6},{6,10},{10,14},{3,7},{... | collective-permute-start | bytes 147464 | tf_op jit(solution)/shard_map/ppermute | solution.py:39
  2891.2 98.1 %collective-permute-start.15 = (bf16[1,3,64,128]{2,3,1,0:T(8,128)(2,1)}, bf16[1,3,64,128]{2,3,1,0:T(8,128)(2,1)}, u32[]{:S(2)}, u32[]{:S(2)}) collective-permute-start(bf16[1,3,64,128]{2,3,1,0:T(8,128)(2,1)} %bitcast.326), channel_id=1, source_target_pairs={{4,0},{8,4},{12,8},{5,1},{9,5},{13,9},{6,2},{10,6},{14,10},{7,3},{... | collective-permute-start | bytes 147464 | tf_op jit(solution)/shard_map/ppermute | solution.py:42
  2988.9 149.8 %all-reduce.81.cloned.1.call-start = ((), (), s32[]{:S(2)}) async-start(), calls=%async_computation.28 | async-start | bytes 6291456
  3051.6 227.0 %all-reduce.93.cloned.1.call-start = ((), (), s32[]{:S(2)}) async-start(), calls=%async_computation.34 | async-start | bytes 7077888 | tf_op jit(solution)/shard_map/psum | solution.py:625
  3069.6 253.8 %all-gather.50.cloned.1.call-start = ((), (), s32[]{:S(2)}) async-start(), calls=%async_computation.20 | async-start | bytes 3932160 | tf_op jit(solution)/shard_map/all_gather | solution.py:85
  (337 other events, 6908.0 us)
Sparse Core Ops, SparseCore 0:
  13.9 41.6 all-reduce.60
  165.1 85.7 all-reduce.66
  253.6 43.9 all-gather.27
  326.2 87.1 all-reduce.68
  416.1 43.9 all-gather.29
  490.9 39.1 all-reduce.62
  673.9 84.7 all-reduce.70
  761.5 43.9 all-gather.31
  843.7 87.1 all-reduce.72
  933.6 43.9 all-gather.33
  1036.9 39.9 all-reduce.64
  1229.1 136.3 all-reduce.84
  1368.3 43.9 all-gather.39
  1414.7 43.9 all-gather.35
  1679.9 36.4 all-reduce.90
  1743.9 138.5 all-reduce.82
  1885.1 43.9 all-gather.37
  1931.6 43.9 all-gather.41
  2017.4 87.1 all-reduce.74
  2107.4 43.9 all-gather.43
  2385.2 35.2 all-reduce.88
  2448.0 86.9 all-reduce.76
  2537.7 43.9 all-gather.45
  2621.1 87.1 all-reduce.78
  2711.2 43.9 all-gather.47
  2989.1 35.1 all-reduce.86
  3051.7 86.9 all-reduce.80
  3143.0 135.5 all-reduce.92
  3280.6 42.7 all-gather.49
where the time goes:
time: 3390 us; the launch traced here: 3370 us
  waiting for transfers between devices  1610 us (47%)
  local copies, waits for them, and re-layouts  688 us (20%)
  blocking collectives  345 us (10%)
  matrix products  334 us (10%)
  other arithmetic  300 us (9%)
  starting transfers between devices  78 us (2%)
    unnamed x39, waiting for transfers between devices  938 us
    all_gather x12, waiting for transfers between devices, tensor_total(): return lax.all_gather(shares, 'tensor', axis=2, tiled=True)  417 us
    all_gather x9, blocking collectives, joined(): gathered = jax.tree.map(lambda a: lax.all_gather(a, axis), part)  192 us
    unnamed x707, local copies, waits for them, and re-layouts  140 us
    psum x3, blocking collectives, broadcast(): return lax.psum(block, axis)  135 us
    psum x1, waiting for transfers between devices, body(): lax.psum(shortened(totals), 'wide')  129 us
    all_gather x12, local copies, waits for them, and re-layouts, tensor_total(): return lax.all_gather(shares, 'tensor', axis=2, tiled=True)  102 us
    psum x3, waiting for transfers between devices, attend_back(): dq_total, glob_total = lax.psum((dq_glob, glob_part), 'wide')  101 us
  transfers between devices with their start and end apart: 51, of which 31 were waited for; matrix products, arithmetic and copies ran while one was open for 15% of the time, Pallas kernels for 0%

commit v1 on v0

v1 whole, which is shorter than its diff:
```python
import functools

import jax
import jax.numpy as jnp
from jax import lax
from jax.experimental import pallas as pl
from jax.experimental.pallas import tpu as pltpu
from jax.sharding import PartitionSpec as P

HW = 64
BLK = 64
EPS = 1e-06
NEG = -1e30
MESH = pl.DeviceIdType.MESH
F32 = jnp.float32
BF16 = jnp.bfloat16
VMEM_BYTES = 56 * 1024 * 1024
GELU_C = 0.7978845608
GELU_A = 0.044715
NT_DIMS = (((1,), (1,)), ((), ()))
TN_DIMS = (((0,), (0,)), ((), ()))
ORDER = (3, 1, 2)
PIECE = 144
LAG = 1


def dot(a, b):
    return jnp.dot(a, b, preferred_element_type=F32)


def dot_nt(a, b):
    return lax.dot_general(a, b, NT_DIMS, preferred_element_type=F32)


def dot_tn(a, b):
    return lax.dot_general(a, b, TN_DIMS, preferred_element_type=F32)


def vmem():
    return pl.BlockSpec(memory_space=pltpu.VMEM)


def anywhere():
    return pl.BlockSpec(memory_space=pl.ANY)


def whole(*shape):
    return pl.BlockSpec(shape, lambda i: (0,) * len(shape))


def of_layer(array, layer):
    return pl.BlockSpec((None,) + array.shape[1:], lambda i: (layer,) + (0,) * (array.ndim - 1))


def remote(src, dst, send_sem, recv_sem, device):
    return pltpu.make_async_remote_copy(
        src_ref=src,
        dst_ref=dst,
        send_sem=send_sem,
        recv_sem=recv_sem,
        device_id=device,
        device_id_type=MESH,
    )


def tensor_peer(me, offset):
    if offset == 1:
        return me + 1 - 2 * lax.rem(me, 2)
    if offset == 2:
        return lax.rem(me + 2, 4)
    return 3 - me


def tensor_barrier(me):
    barrier = pltpu.get_barrier_semaphore()
    for offset in (1, 2, 3):
        pl.semaphore_signal(
            barrier, inc=1, device_id={"tensor": tensor_peer(me, offset)}, device_id_type=MESH
        )
    return barrier


def params(collective_id=None):
    if collective_id is None:
        return pltpu.CompilerParams(vmem_limit_bytes=VMEM_BYTES)
    return pltpu.CompilerParams(
        vmem_limit_bytes=VMEM_BYTES, collective_id=collective_id, has_side_effects=True
    )


def key_blocks(ids_ref, layer, head, row, first, total):
    b = first + row
    start = jnp.clip(b - 1, 0, total - 3)
    window = [start, start + 1, start + 2]
    r = [ids_ref[layer, head, b * 3 + k] for k in range(3)]

    def far(block):
        return (block < b - 1) | (block > b + 1)

    fresh = [far(k) & (k >= 2) for k in r]
    allowed = [jnp.logical_not(far(k)) for k in window]
    allowed += [far(jnp.int32(0)), far(jnp.int32(1))]
    allowed += [fresh[0], fresh[1] & (r[1] != r[0]), fresh[2] & (r[2] != r[0]) & (r[2] != r[1])]
    return window + [jnp.int32(0), jnp.int32(1)] + r, allowed


def back_blocks(ids_ref, layer, head, b, total):
    blocks, allowed = key_blocks(ids_ref, layer, head, 0, b, total)
    window = [jnp.maximum(b - 1, 0), b, jnp.minimum(b + 1, total - 1)]
    return window + blocks[3:], [b >= 1, b >= 0, b + 1 < total] + allowed[3:]


def key_bias(blocks, allowed, length):
    lane = lax.broadcasted_iota(jnp.int32, (1, 8 * BLK), 1)
    slot = lane // BLK
    limit = jnp.zeros((1, 8 * BLK), jnp.int32)
    for s in range(8):
        tokens = jnp.where(allowed[s], jnp.clip(length - blocks[s] * BLK, 0, BLK), 0)
        limit = jnp.where(slot == s, tokens, limit)
    return jnp.where(lane - slot * BLK < limit, 0.0, NEG)


def gathered(kv_ref, blocks):
    window = kv_ref[pl.ds(blocks[0], 3)].reshape(3 * BLK, -1)
    ends = kv_ref[0:2].reshape(2 * BLK, -1)
    return jnp.concatenate([window, ends] + [kv_ref[k] for k in blocks[5:]], axis=0)


def grouping(rows_here):
    return max(u for u in (4, 3, 2, 1) if rows_here % u == 0)


def wide_barrier(me, count):
    barrier = pltpu.get_barrier_semaphore()
    for side in (1, count - 1):
        pl.semaphore_signal(
            barrier,
            inc=1,
            device_id={"wide": lax.rem(me + side, count)},
            device_id_type=MESH,
        )
    return barrier


def softmax_values(s, keys):
    peak = jnp.max(s, axis=-1, keepdims=True)
    e = jnp.exp(s - peak)
    mass = jnp.sum(e, axis=-1, keepdims=True)
    return dot(e.astype(BF16), keys) / mass, peak + jnp.log(mass)


def gather_attend(
    count, heads, layer, x_ref, wt_ref, bias, ids_ref, len_ref, outs, scratch, ready, finished
):
    q_ref, kv_ref, att_ref, lse_ref, top_ref = outs
    held, (save, send_r, recv_r, send_l, recv_l) = scratch[:heads], scratch[heads:]
    me = lax.axis_index("wide")
    tok = x_ref.shape[0]
    right, left = {"wide": lax.rem(me + 1, count)}, {"wide": lax.rem(me + count - 1, count)}
    pair = 2 * HW
    wide = heads * pair
    has_right, has_left = me < count - 1, me > 0
    length = len_ref[0]
    rows_here = tok // BLK
    total = held[0].shape[0]
    unit = grouping(rows_here)
    groups = rows_here // unit

    def rows(shard):
        return pl.ds(shard * rows_here, rows_here)

    kv = dot_nt(x_ref[...], wt_ref[wide:, :]) + bias[:, wide:]
    for h in range(heads):
        own = kv[:, h * pair : (h + 1) * pair].astype(BF16)
        held[h][rows(me)] = own.reshape(rows_here, BLK, pair)
    ready()

    def copy_r(h, shard, step):
        part = held[h].at[rows(shard)]
        return remote(part, part, send_r.at[h, step], recv_r.at[h, shard], right)

    def copy_l(h, shard, step):
        part = held[h].at[rows(shard)]
        return remote(part, part, send_l.at[h, step], recv_l.at[h, shard], left)

    for h in range(heads):

        @pl.when(has_right)
        def _():
            copy_r(h, me, 0).start()

        @pl.when(has_left)
        def _():
            copy_l(h, me, 0).start()

    q = dot_nt(x_ref[...], wt_ref[:wide, :]) + bias[:, :wide]
    q_ref[...] = q.astype(BF16)

    def forward(h, step):
        shard_r, shard_l = me - step, me + step

        @pl.when(shard_r >= 0)
        def _():
            copy_r(h, shard_r, step).wait_recv()

            @pl.when(has_right)
            def _():
                copy_r(h, shard_r, step).start()

        @pl.when(shard_l < count)
        def _():
            copy_l(h, shard_l, step).wait_recv()

            @pl.when(has_left)
            def _():
                copy_l(h, shard_l, step).start()

    def forward_from(h, first):
        def step(k, carry):
            forward(h, k)
            return carry

        lax.fori_loop(first, count, step, 0)

    forward_from(0, 1)
    for h in range(heads):
        pltpu.make_async_copy(held[h], kv_ref.at[h], save.at[h]).start()
        cols = slice(h * pair, (h + 1) * pair)

        def group(g, carry):
            for u in range(unit):
                row = g * unit + u
                here = pl.ds(pl.multiple_of(row * BLK, BLK), BLK)
                blocks, allowed = key_blocks(ids_ref, layer, h, row, me * rows_here, total)
                keys = gathered(held[h], blocks)
                s = dot_nt(q_ref[here, cols], keys) + key_bias(blocks, allowed, length)
                o, lse = softmax_values(s, keys)
                att_ref[here, cols] = o.astype(BF16)
                lse_ref[h, here, :] = lse
            if h + 1 < heads:

                @pl.when(g + 1 < count)
                def _():
                    forward(h + 1, g + 1)

            return carry

        lax.fori_loop(0, groups, group, 0)
        if h + 1 < heads:
            forward_from(h + 1, groups + 1)

        @pl.when(me == 0)
        def _():
            keys = held[h][...].reshape(total * BLK, pair)
            token = lax.broadcasted_iota(jnp.int32, (1, keys.shape[0]), 1)
            s = dot_nt(q_ref[0 : 2 * BLK, cols], keys) + jnp.where(token < length, 0.0, NEG)
            o, lse = softmax_values(s, keys)
            att_ref[0 : 2 * BLK, cols] = o.astype(BF16)
            lse_ref[h, 0 : 2 * BLK, :] = lse
            top_ref[h] = o

        @pl.when(me != 0)
        def _():
            top_ref[h] = jnp.zeros((2 * BLK, pair), F32)

    finished()

    def drain(step, carry):
        shard_r, shard_l = me - step, me + step
        for h in range(heads):

            @pl.when((shard_r >= 0) & has_right)
            def _():
                copy_r(h, shard_r, step).wait_send()

            @pl.when((shard_l < count) & has_left)
            def _():
                copy_l(h, shard_l, step).wait_send()

        return carry

    lax.fori_loop(0, count, drain, 0)
    for h in range(heads):
        pltpu.make_async_copy(held[h], kv_ref.at[h], save.at[h]).wait()


def attend_outs(count, heads, tok):
    pair = 2 * HW
    shapes = [
        jax.ShapeDtypeStruct((tok, heads * pair), BF16),
        jax.ShapeDtypeStruct((heads, count * tok // BLK, BLK, pair), BF16),
        jax.ShapeDtypeStruct((tok, heads * pair), BF16),
        jax.ShapeDtypeStruct((heads, tok, 1), F32),
        jax.ShapeDtypeStruct((heads, 2 * BLK, pair), F32),
    ]
    specs = [anywhere() if i == 1 else whole(*a.shape) for i, a in enumerate(shapes)]
    return shapes, specs


def gather_scratch(count, heads, tok):
    return (
        [pltpu.VMEM((count * tok // BLK, BLK, 2 * HW), BF16)] * heads
        + [pltpu.SemaphoreType.DMA((heads,))]
        + [pltpu.SemaphoreType.DMA((heads, count))] * 4
    )


def scalars():
    return pl.BlockSpec(memory_space=pltpu.SMEM)


def begin_kernel(
    count,
    heads,
    ids_ref,
    len_ref,
    inputs_ref,
    wq_ref,
    wk_ref,
    wv_ref,
    win_ref,
    wffn_ref,
    wout_ref,
    bq_ref,
    bv_ref,
    bout_ref,
    g1_ref,
    b1_ref,
    bin_ref,
    bffn_ref,
    g2_ref,
    b2_ref,
    x_ref,
    q_ref,
    kv_ref,
    att_ref,
    lse_ref,
    top_ref,
    wt_ref,
    vall_ref,
    win_all_ref,
    wffn_all_ref,
    wout_all_ref,
    turn,
    x_sem,
    keep,
    send,
    recv,
    *scratch,
):
    section = lax.axis_index("section")
    other = {"section": 1 - section}
    barrier = wide_barrier(lax.axis_index("wide"), count)
    pl.semaphore_signal(barrier, inc=1, device_id=other, device_id_type=MESH)
    load = pltpu.make_async_copy(inputs_ref.at[section, 0], x_ref, x_sem)
    load.start()
    wide = heads * 2 * HW
    scale = jnp.asarray(0.125, BF16)
    none = jnp.zeros((HW, x_ref.shape[1]), BF16)
    row = []
    for h in range(heads):
        at, cut = h * 2 * HW, slice(h * HW, (h + 1) * HW)
        wt_ref[section, at : at + HW, :] = wq_ref[cut, :] * scale
        wt_ref[section, at + HW : at + 2 * HW, :] = none
        wt_ref[section, wide + at : wide + at + HW, :] = wk_ref[cut, :]
        wt_ref[section, wide + at + HW : wide + at + 2 * HW, :] = wv_ref[cut, :]
        row += [bq_ref[:, cut].astype(F32) * 0.125, jnp.zeros((1, HW), F32)]
    for h in range(heads):
        row += [jnp.zeros((1, HW), F32), bv_ref[:, h * HW : (h + 1) * HW].astype(F32)]
    vall_ref[section, 0:1, :] = jnp.concatenate(row, axis=1)
    for i, ref in enumerate((bout_ref, g1_ref, b1_ref, bin_ref, bffn_ref, g2_ref, b2_ref)):
        vall_ref[section, i + 1 : i + 2, :] = ref[...].astype(F32)
    pl.semaphore_wait(barrier, 3)

    pairs = [
        (wt_ref.at[section], wt_ref.at[section]),
        (vall_ref.at[section], vall_ref.at[section]),
        (win_ref, win_all_ref.at[section]),
        (wffn_ref, wffn_all_ref.at[section]),
        (wout_ref, wout_all_ref.at[section]),
    ]
    swaps = [remote(src, dst, send.at[i], recv.at[i], other) for i, (src, dst) in enumerate(pairs)]
    keeps = [
        pltpu.make_async_copy(src, dst, keep.at[i]) for i, (src, dst) in enumerate(pairs[2:])
    ]
    for copy in swaps + keeps:
        copy.start()
    load.wait()

    @pl.when(section == 1)
    def _():
        swaps[0].wait_recv()
        swaps[1].wait_recv()

    def ready():
        @pl.when(section == 1)
        def _():
            pl.semaphore_wait(turn, 1)

    def finished():
        @pl.when(section == 0)
        def _():
            pl.semaphore_signal(turn, inc=1, device_id={"section": 1}, device_id_type=MESH)

    gather_attend(
        count,
        heads,
        0,
        x_ref,
        wt_ref.at[0],
        vall_ref[0, 0:1, :],
        ids_ref,
        len_ref,
        (q_ref, kv_ref, att_ref, lse_ref, top_ref),
        scratch,
        ready,
        finished,
    )

    @pl.when(section == 0)
    def _():
        swaps[0].wait_recv()
        swaps[1].wait_recv()

    for copy in swaps[2:]:
        copy.wait_recv()
    for copy in swaps:
        copy.wait_send()
    for copy in keeps:
        copy.wait()


def begin(ids, length, inputs, matrices, vectors, count, heads, collective_id):
    _, _, tok, width = inputs.shape
    wide = heads * 2 * HW
    narrow = heads * HW
    both = [(2, width, width), (2, width, width), (2, narrow, width)]
    shapes, specs = attend_outs(count, heads, tok)
    return pl.pallas_call(
        functools.partial(begin_kernel, count, heads),
        grid=(1,),
        out_shape=[jax.ShapeDtypeStruct((tok, width), BF16)]
        + shapes
        + [
            jax.ShapeDtypeStruct((2, 2 * wide, width), BF16),
            jax.ShapeDtypeStruct((2, 8, width), F32),
        ]
        + [jax.ShapeDtypeStruct(shape, BF16) for shape in both],
        in_specs=[scalars(), scalars(), anywhere()]
        + [whole(*m.shape) for m in matrices]
        + [whole(*v.shape) for v in vectors],
        out_specs=[whole(tok, width)]
        + specs
        + [whole(2, 2 * wide, width), whole(2, 8, width)]
        + [anywhere()] * 3,
        scratch_shapes=[
            pltpu.SemaphoreType.REGULAR,
            pltpu.SemaphoreType.DMA,
            pltpu.SemaphoreType.DMA((3,)),
            pltpu.SemaphoreType.DMA((5,)),
            pltpu.SemaphoreType.DMA((5,)),
        ]
        + gather_scratch(count, heads, tok),
        compiler_params=params(collective_id),
        name="begin",
    )(ids, length, inputs, *matrices, *vectors)


def project_kernel(count, heads, layer, ids_ref, len_ref, x_ref, wt_ref, v_ref, *refs):
    barrier = wide_barrier(lax.axis_index("wide"), count)
    gather_attend(
        count,
        heads,
        layer,
        x_ref,
        wt_ref,
        v_ref[0:1, :],
        ids_ref,
        len_ref,
        refs[:5],
        refs[5:],
        lambda: pl.semaphore_wait(barrier, 2),
        lambda: None,
    )


def project(ids, length, x, wt, vall, layer, count, heads, collective_id):
    tok, width = x.shape
    shapes, specs = attend_outs(count, heads, tok)
    return pl.pallas_call(
        functools.partial(project_kernel, count, heads, layer),
        grid=(1,),
        out_shape=shapes,
        in_specs=[scalars(), scalars(), whole(tok, width), of_layer(wt, layer), of_layer(vall, layer)],
        out_specs=specs,
        scratch_shapes=gather_scratch(count, heads, tok),
        compiler_params=params(collective_id),
        name="project",
    )(ids, length, x, wt, vall)


class Square:
    def __init__(self, me, own, width, blocks, send_buf, recv_buf, hold, send_sem, recv_sem):
        self.me = me
        self.x, self.y, self.d = (tensor_peer(me, k) for k in (1, 2, 3))
        self.own, self.sub, self.half = own, own // blocks, width // 2
        self.blocks = blocks
        self.send_buf, self.recv_buf, self.hold = send_buf, recv_buf, hold
        self.send_sem, self.recv_sem = send_sem, recv_sem
        self.used = []

    def rows(self, index, j, size=None):
        return pl.ds(pl.multiple_of(index * self.own + j * self.sub, 16), size or self.sub)

    def to(self, m):
        return {"tensor": self.x if m < 3 else self.y}

    def scatter(self, stage, j, m):
        slot = self.scatters.index(stage)
        return remote(
            self.send_buf.at[slot, j, m],
            self.recv_buf.at[slot, j, m],
            self.send_sem.at[stage, j, m],
            self.recv_sem.at[stage, j, m],
            self.to(m),
        )

    def put(self, stage, j, m, value):
        self.send_buf[self.scatters.index(stage), j, m] = value.astype(BF16)
        self.scatter(stage, j, m).start()
        self.used.append(self.scatter(stage, j, m))

    def got(self, stage, j, m):
        self.scatter(stage, j, m).wait_recv()
        return self.recv_buf[self.scatters.index(stage), j, m].astype(F32)

    def give_diagonal(self, stage, j, part):
        self.put(stage, j, 0, part[:, self.half :])
        self.put(stage, j, 3, part[:, : self.half])

    def give_x(self, stage, j, part):
        self.put(stage, j, 1, part[:, self.half :])
        self.hold[j, 0] = part[:, : self.half]

    def give_y(self, stage, j, part):
        self.put(stage, j, 4, part[:, : self.half])
        self.hold[j, 1] = part[:, self.half :]

    def relay_sum(self, stage, j):
        self.put(stage, j, 2, self.hold[j, 0] + self.got(stage, j, 3))
        self.put(stage, j, 5, self.hold[j, 1] + self.got(stage, j, 0))

    def total(self, stage, j, own):
        left = own[:, : self.half] + self.got(stage, j, 4) + self.got(stage, j, 2)
        right = own[:, self.half :] + self.got(stage, j, 1) + self.got(stage, j, 5)
        return jnp.concatenate([left, right], axis=1)

    def gather(self, stage, j, m, ref, index, first):
        cols = pl.ds(0 if first else self.half, self.half)
        return remote(
            ref.at[self.rows(index, j), cols],
            ref.at[self.rows(index, j), cols],
            self.send_sem.at[stage, j, m],
            self.recv_sem.at[stage, j, m],
            self.to(m),
        )

    def send(self, copy):
        copy.start()
        self.used.append(copy)

    def share(self, stage, j, ref):
        for m, first in ((0, True), (3, False), (1, False), (4, True)):
            self.send(self.gather(stage, j, m, ref, self.me, first))

    def relay_share(self, stage, j, ref):
        self.gather(stage, j, 0, ref, self.x, True).wait_recv()
        self.send(self.gather(stage, j, 5, ref, self.x, True))
        self.gather(stage, j, 3, ref, self.y, False).wait_recv()
        self.send(self.gather(stage, j, 2, ref, self.y, False))

    def have_x(self, stage, j, ref):
        self.gather(stage, j, 1, ref, self.x, False).wait_recv()

    def have_y(self, stage, j, ref):
        self.gather(stage, j, 4, ref, self.y, True).wait_recv()

    def have_diagonal(self, stage, j, ref):
        self.gather(stage, j, 5, ref, self.d, True).wait_recv()
        self.gather(stage, j, 2, ref, self.d, False).wait_recv()

    def have_all(self, stage, j, ref):
        self.have_x(stage, j, ref)
        self.have_y(stage, j, ref)
        self.have_diagonal(stage, j, ref)

    def close(self):
        for copy in self.used:
            copy.wait_send()


def square_barrier(me):
    barrier = pltpu.get_barrier_semaphore()
    for offset in (1, 2):
        pl.semaphore_signal(
            barrier, inc=1, device_id={"tensor": tensor_peer(me, offset)}, device_id_type=MESH
        )
    return barrier


def sub_blocks(own):
    return 2 if own % 32 == 0 else 1


def square_scratch(scatters, stages, own, width):
    blocks = sub_blocks(own)
    buf = pltpu.VMEM((scatters, blocks, 6, own // blocks, width // 2), BF16)
    return [
        buf,
        buf,
        pltpu.VMEM((blocks, 2, own // blocks, width // 2), F32),
        pltpu.SemaphoreType.DMA((stages, blocks, 6)),
        pltpu.SemaphoreType.DMA((stages, blocks, 6)),
    ]


def norm_parts(values):
    center = values - jnp.mean(values, axis=-1, keepdims=True)
    rstd = lax.rsqrt(jnp.mean(center * center, axis=-1, keepdims=True) + EPS)
    return center * rstd, rstd


def dense_kernel(
    last,
    layer,
    att_ref,
    x_ref,
    wout_ref,
    v_ref,
    win_any,
    wffn_any,
    mixed_any,
    active_any,
    slope_any,
    r1_ref,
    r2_ref,
    out_ref,
    wout_pad,
    win_ref,
    wffn_ref,
    mixed_ref,
    active_ref,
    slope_ref,
    sems,
    *scratch,
):
    me = lax.axis_index("tensor")
    own, width = x_ref.shape[0] // 4, x_ref.shape[1]
    blocks = sub_blocks(own)
    barrier = square_barrier(me)
    sq = Square(me, own, width, blocks, *scratch)
    pad_heads(wout_ref, wout_pad)
    sq.scatters = (0, 2)
    loads = [
        pltpu.make_async_copy(src.at[layer], dst, sems.at[i])
        for i, (src, dst) in enumerate(((win_any, win_ref), (wffn_any, wffn_ref)))
    ]
    for load in loads:
        load.start()
    stores = [
        pltpu.make_async_copy(src, dst, sems.at[2 + i])
        for i, (src, dst) in enumerate(
            ((mixed_ref, mixed_any), (active_ref, active_any), (slope_ref, slope_any))
        )
    ]

    def local(j):
        return slice(j * sq.sub, (j + 1) * sq.sub)

    def branch(index, j):
        return dot(att_ref[sq.rows(index, j), :], wout_pad[...])

    for j in range(blocks):
        part = branch(sq.d, j)
        if j == 0:
            pl.semaphore_wait(barrier, 2)
        sq.give_diagonal(0, j, part)
    for j in range(blocks):
        sq.give_x(0, j, branch(sq.x, j))
        sq.give_y(0, j, branch(sq.y, j))
    for j in range(blocks):
        r1_ref[local(j), :] = (
            branch(me, j) + x_ref[sq.rows(me, j), :].astype(F32) + v_ref[1:2, :]
        )
        sq.relay_sum(0, j)
    for j in range(blocks):
        total = sq.total(0, j, r1_ref[local(j), :])
        r1_ref[local(j), :] = total
        mixed = (norm_parts(total)[0] * v_ref[2:3, :] + v_ref[3:4, :]).astype(BF16)
        mixed_ref[sq.rows(me, j), :] = mixed
        sq.share(1, j, mixed_ref)

    for load in loads:
        load.wait()

    def feed(index, j):
        here = sq.rows(index, j)
        u = dot(mixed_ref[here, :], win_ref[...]) + v_ref[4:5, :]
        th = jnp.tanh(GELU_C * (u + GELU_A * u * u * u))
        half = 0.5 * (1.0 + th)
        slope = half + 0.5 * u * (1.0 - th * th) * (GELU_C * (1.0 + 3.0 * GELU_A * u * u))
        slope_ref[here, :] = slope.astype(BF16)
        active = (u * half).astype(BF16)
        active_ref[here, :] = active
        return dot(active, wffn_ref[...])

    for j in range(blocks):
        r2_ref[local(j), :] = (
            feed(me, j) + mixed_ref[sq.rows(me, j), :].astype(F32) + v_ref[5:6, :]
        )
        sq.relay_share(1, j, mixed_ref)
    for j in range(blocks):
        sq.have_x(1, j, mixed_ref)
        sq.give_x(2, j, feed(sq.x, j))
        sq.have_y(1, j, mixed_ref)
        sq.give_y(2, j, feed(sq.y, j))
        sq.have_diagonal(1, j, mixed_ref)
        sq.give_diagonal(2, j, feed(sq.d, j))
    for store in stores:
        store.start()
    for j in range(blocks):
        sq.relay_sum(2, j)
    for j in range(blocks):
        total = sq.total(2, j, r2_ref[local(j), :])
        r2_ref[local(j), :] = total
        result = (norm_parts(total)[0] * v_ref[6:7, :] + v_ref[7:8, :]).astype(BF16)
        if last:
            out_ref[local(j), :] = result
        else:
            out_ref[sq.rows(me, j), :] = result
            sq.share(3, j, out_ref)
    if not last:
        for j in range(blocks):
            sq.relay_share(3, j, out_ref)
        for j in range(blocks):
            sq.have_all(3, j, out_ref)
    sq.close()
    for store in stores:
        store.wait()


def pad_heads(rows_ref, padded_ref):
    for h in range(rows_ref.shape[0] // HW):
        at = h * 2 * HW
        padded_ref[at : at + HW, :] = jnp.zeros((HW, rows_ref.shape[1]), rows_ref.dtype)
        padded_ref[at + HW : at + 2 * HW, :] = rows_ref[h * HW : (h + 1) * HW, :]


def dense(att, x, wout, win, wffn, vall, layer, collective_id):
    tok, width = x.shape
    own = tok // 4
    wide = att.shape[1]
    last = layer == 1
    out_rows = own if last else tok
    return pl.pallas_call(
        functools.partial(dense_kernel, last, layer),
        out_shape=[jax.ShapeDtypeStruct((tok, width), BF16)] * 3
        + [jax.ShapeDtypeStruct((own, width), F32)] * 2
        + [jax.ShapeDtypeStruct((out_rows, width), BF16)],
        grid=(1,),
        in_specs=[whole(tok, wide), whole(tok, width)]
        + [of_layer(a, layer) for a in (wout, vall)]
        + [anywhere()] * 2,
        out_specs=[anywhere()] * 3 + [whole(own, width)] * 2 + [whole(out_rows, width)],
        scratch_shapes=[
            pltpu.VMEM((wide, width), BF16),
            pltpu.VMEM((width, width), BF16),
            pltpu.VMEM((width, width), BF16),
            pltpu.VMEM((tok, width), BF16),
            pltpu.VMEM((tok, width), BF16),
            pltpu.VMEM((tok, width), BF16),
            pltpu.SemaphoreType.DMA((5,)),
        ]
        + square_scratch(2, 4, own, width),
        compiler_params=params(collective_id),
        name="dense",
    )(att, x, wout, vall, win, wffn)


def norm_back(values, grad, gain):
    n, rstd = norm_parts(values)
    f = grad * gain
    back = (
        f - jnp.mean(f, axis=-1, keepdims=True) - n * jnp.mean(f * n, axis=-1, keepdims=True)
    ) * rstd
    return back, n


def dense_back_kernel(
    count,
    with_chain,
    g_ref,
    weight_ref,
    r2_ref,
    r1_ref,
    wout_ref,
    v_ref,
    *refs,
):
    late_any, refs = refs[:6], refs[6:]
    if with_chain:
        old_any, gqkv_ref, refs = refs[0], refs[1], refs[2:]
    gw_ref, gv_ref, do_ref, dr1_ref = refs[:4]
    refs = refs[4:]
    if with_chain:
        up_ref, gqkv_sum, refs = refs[0], refs[1], refs[2:]
    late, late_sems = refs[:6], refs[6]
    wffn_ref, slope_ref, win_ref, active_ref, mixed_ref, att_ref = late
    refs = refs[7:]
    layer = 0 if with_chain else 1
    loads = [
        pltpu.make_async_copy(src.at[layer] if i in (0, 2) else src, dst, late_sems.at[i])
        for i, (src, dst) in enumerate(zip(late_any, late))
    ]
    for load in loads:
        load.start()
    db2, dh, db1, wout_pad, g_buf, g_sem = refs[:6]
    refs = refs[3:]
    me = lax.axis_index("tensor")
    wide_at = lax.axis_index("wide")
    section = lax.axis_index("section")
    own, width = r1_ref.shape
    wide = att_ref.shape[1]
    blocks = sub_blocks(own)
    barrier = square_barrier(me)
    sq = Square(me, own, width, blocks, *refs[3:8])
    sq.scatters = (1,)
    refs = refs[8:]
    if with_chain:
        old, old_sem, sems, landed, hand_sems, ready = refs
        line = Line(count)
        rows = old.shape[0]
        half = gqkv_sum.shape[0]

        def half_of(core):
            return pl.ds(pl.multiple_of(core * half, 16), half)

        def swap():
            return remote(
                gqkv_ref.at[half_of(1 - section)],
                landed,
                hand_sems.at[0],
                hand_sems.at[1],
                {"section": 1 - section},
            )

        load_old = pltpu.make_async_copy(
            old_any.at[pl.ds(pl.multiple_of(section * rows, 16), rows)], old, old_sem
        )
        load_old.start()
        for side in (1, count - 1):
            pl.semaphore_signal(
                barrier,
                inc=1,
                device_id={"wide": lax.rem(wide_at + side, count)},
                device_id_type=MESH,
            )

        def inwards(source):
            return remote(source, up_ref, sems.at[0], sems.at[1], line.inward)

    def down(values):
        return jnp.sum(values, axis=0, keepdims=True)

    def local(j):
        return slice(j * sq.sub, (j + 1) * sq.sub)

    if with_chain:

        def gradient(j):
            return g_ref[local(j), :].astype(F32)

    else:
        load = pltpu.make_async_copy(g_ref.at[section, 0, sq.rows(me, 0, own)], g_buf, g_sem)
        load.start()
        weight = weight_ref[section]
        count_all = jnp.sum(jnp.sum(weight, axis=1, keepdims=True), axis=0, keepdims=True)
        factor = (weight.shape[0] * weight.shape[1]) / count_all
        here = weight_ref[section, pl.ds(wide_at * 4 + me, 1), :]
        equal = lax.broadcasted_iota(jnp.int32, (own, own), 0) == lax.broadcasted_iota(
            jnp.int32, (own, own), 1
        )
        column = jnp.sum(jnp.where(equal, here, 0.0), axis=1, keepdims=True) * factor
        load.wait()

        def gradient(j):
            return g_buf[local(j), :].astype(F32) * column[local(j), :]

    pad_heads(wout_ref, wout_pad)
    d_gain, d_shift, d_bias = 0.0, 0.0, 0.0
    for j in range(blocks):
        grad = gradient(j)
        d_two, n_two = norm_back(r2_ref[local(j), :], grad, v_ref[6:7, :])
        db2[sq.rows(me, j), :] = d_two.astype(BF16)
        dr1_ref[local(j), :] = d_two
        if j == 0:
            if with_chain:
                greet(barrier, section, 4)
                tell_ready(ready, section)
            else:
                pl.semaphore_wait(barrier, 2)
        sq.share(0, j, db2)
        d_gain += down(grad * n_two)
        d_shift += down(grad)
        d_bias += down(d_two)
    gv_ref[6:7, :] = d_gain
    gv_ref[7:8, :] = d_shift
    gv_ref[5:6, :] = d_bias

    def feed(index, j):
        here = sq.rows(index, j)
        back = dot_nt(db2[here, :], wffn_ref[...]) * slope_ref[here, :].astype(F32)
        low = back.astype(BF16)
        dh[here, :] = low
        return dot_nt(low, win_ref[...])

    if with_chain:
        load_old.wait()

        @pl.when(line.no_outer)
        def _():
            inwards(old).start()

        @pl.when(section == 1)
        def _():
            swap().start()

    for load in loads[:3]:
        load.wait()
    for j in range(blocks):
        dr1_ref[local(j), :] += feed(me, j)
        sq.relay_share(0, j, db2)
    for j in range(blocks):
        sq.have_x(0, j, db2)
        sq.give_x(1, j, feed(sq.x, j))
        sq.have_y(0, j, db2)
        sq.give_y(1, j, feed(sq.y, j))
        sq.have_diagonal(0, j, db2)
        sq.give_diagonal(1, j, feed(sq.d, j))
    for j in range(blocks):
        sq.relay_sum(1, j)
    for load in loads[3:]:
        load.wait()
    step = 256
    for i in range(width // step):
        cols = slice(i * step, (i + 1) * step)
        gw_ref[width + i * step : width + (i + 1) * step, :] = dot_tn(
            active_ref[:, cols], db2[...]
        ).astype(BF16)
        gw_ref[cols, :] = dot_tn(mixed_ref[:, cols], dh[...]).astype(BF16)
    gv_ref[4:5, :] = down(dh[...].astype(F32))
    d_gain, d_shift, d_bias = 0.0, 0.0, 0.0
    for j in range(blocks):
        total = sq.total(1, j, dr1_ref[local(j), :])
        d_one, n_one = norm_back(r1_ref[local(j), :], total, v_ref[2:3, :])
        db1[sq.rows(me, j), :] = d_one.astype(BF16)
        sq.share(2, j, db1)
        dr1_ref[local(j), :] = d_one
        d_gain += down(total * n_one)
        d_shift += down(total)
        d_bias += down(d_one)
    gv_ref[2:3, :] = d_gain
    gv_ref[3:4, :] = d_shift
    gv_ref[1:2, :] = d_bias
    gv_ref[0:1, :] = jnp.zeros((1, width), F32)

    def attended_back(index, j):
        here = sq.rows(index, j)
        do_ref[here, :] = dot_nt(db1[here, :], wout_pad[...]).astype(BF16)

    for j in range(blocks):
        attended_back(me, j)
        sq.relay_share(2, j, db1)
    for j in range(blocks):
        sq.have_x(2, j, db1)
        attended_back(sq.x, j)
        sq.have_y(2, j, db1)
        attended_back(sq.y, j)
        sq.have_diagonal(2, j, db1)
        attended_back(sq.d, j)
    for h in range(wide // (2 * HW)):
        cols = slice(h * 2 * HW, (h + 1) * 2 * HW)
        gw_ref[2 * width + h * HW : 2 * width + (h + 1) * HW, :] = dot_tn(
            att_ref[:, cols], db1[...]
        )[HW:].astype(BF16)
    sq.close()
    if with_chain:
        await_ready(ready, section)

        @pl.when(section == 0)
        def _():
            swap().start()

        @pl.when(line.has_outer)
        def _():
            inwards(old).wait_recv()

            def add(i, carry):
                span = pl.ds(pl.multiple_of(i * PIECE, 16), PIECE)
                up_ref[span, :] = (up_ref[span, :].astype(F32) + old[span, :].astype(F32)).astype(BF16)
                return carry

            lax.fori_loop(0, rows // PIECE, add, 0)

        @pl.when(line.has_outer & line.not_middle)
        def _():
            inwards(up_ref).start()

        @pl.when(line.not_middle)
        def _():
            inwards(old).wait_send()

        swap().wait()
        gqkv_sum[...] = (
            gqkv_ref[half_of(section), :].astype(F32) + landed[...].astype(F32)
        ).astype(BF16)


def dense_back(
    g, weight, r2, r1, slope, active, mixed, att, wout, win, wffn, vall, layer, count, collective_id, old
):
    own, width = r1.shape
    tok, wide = att.shape
    gw_rows = 2 * width + wide // 2
    extra_out, extra_scratch = [], []
    if old:
        half = (old[0].shape[0] // 2, width)
        small = (old[1].shape[0] // 2, width)
        extra_out = [half, small]
        extra_scratch = [
            pltpu.VMEM(half, BF16),
            pltpu.SemaphoreType.DMA,
            pltpu.SemaphoreType.DMA((2,)),
            pltpu.VMEM(small, BF16),
            pltpu.SemaphoreType.DMA((2,)),
            pltpu.SemaphoreType.REGULAR,
        ]
    return pl.pallas_call(
        functools.partial(dense_back_kernel, count, bool(old)),
        out_shape=[
            jax.ShapeDtypeStruct((gw_rows, width), BF16),
            jax.ShapeDtypeStruct((8, width), F32),
            jax.ShapeDtypeStruct((tok, wide), BF16),
            jax.ShapeDtypeStruct((own, width), F32),
        ]
        + [jax.ShapeDtypeStruct(shape, BF16) for shape in extra_out],
        grid=(1,),
        in_specs=[whole(own, width) if old else anywhere(), whole(*weight.shape)]
        + [whole(own, width)] * 2
        + [of_layer(a, layer) for a in (wout, vall)]
        + [anywhere()] * 6
        + ([anywhere(), whole(*old[1].shape)] if old else []),
        out_specs=[
            whole(gw_rows, width),
            whole(8, width),
            whole(tok, wide),
            whole(own, width),
        ]
        + [whole(*shape) for shape in extra_out],
        scratch_shapes=[
            pltpu.VMEM((width, width), BF16),
            pltpu.VMEM((tok, width), BF16),
            pltpu.VMEM((width, width), BF16),
            pltpu.VMEM((tok, width), BF16),
            pltpu.VMEM((tok, width), BF16),
            pltpu.VMEM((tok, wide), BF16),
            pltpu.SemaphoreType.DMA((6,)),
            pltpu.VMEM((tok, width), BF16),
            pltpu.VMEM((tok, width), BF16),
            pltpu.VMEM((tok, width), BF16),
            pltpu.VMEM((wide, width), BF16),
            pltpu.VMEM((own, width), BF16),
            pltpu.SemaphoreType.DMA,
        ]
        + square_scratch(1, 3, own, width)
        + extra_scratch,
        compiler_params=params(collective_id),
        name="dense_back",
    )(g, weight, r2, r1, wout, vall, wffn, slope, win, active, mixed, att, *old)


def attend_back(h, layer, total, scalars_, refs, hook):
    ids_ref, len_ref, perm_ref, start_ref = scalars_
    q_ref, kv_ref, do_ref, lse_ref, top_ref, joined, dkv, acc, rand, sums = refs
    me = lax.axis_index("wide")
    pair = 2 * HW
    rows_here = q_ref.shape[0] // BLK
    unit = grouping(rows_here)
    cols = slice(h * pair, (h + 1) * pair)
    length = len_ref[0]
    first = me * rows_here
    acc[...] = jnp.zeros_like(acc)

    def group(g, carry):
        for u in range(unit):
            row = g * unit + u
            b = first + row
            here = pl.ds(pl.multiple_of(row * BLK, BLK), BLK)
            blocks, allowed = back_blocks(ids_ref, layer, h, b, total)
            keys = jnp.concatenate([kv_ref[h, k] for k in blocks], axis=0)
            keep = jnp.where((me == 0) & (row < 2), 0.0, 1.0).astype(BF16)
            do_here = do_ref[here, cols] * keep
            both = jnp.concatenate([q_ref[here, cols], do_here], axis=0)
            s_dp = dot_nt(both, keys)
            p = jnp.exp(s_dp[:BLK] + key_bias(blocks, allowed, length) - lse_ref[h, here, :])
            p_dp = p * s_dp[BLK:]
            ds = (p_dp - p * jnp.sum(p_dp, axis=-1, keepdims=True)).astype(BF16)
            joined[here, cols] = dot(ds, keys).astype(BF16)
            d_keys = dot_tn(jnp.concatenate([ds, p.astype(BF16)], axis=0), both)
            d_keys = d_keys.reshape(8, BLK, pair)
            acc[pl.ds(b, 3)] += d_keys[:3]
            acc[1:3] += d_keys[3:5]
            rand[pl.ds(row * 3, 3)] = d_keys[5:]
        hook(g)
        return carry

    lax.fori_loop(0, rows_here // unit, group, 0)

    @pl.when(me == 0)
    def _():
        top = slice(0, 2 * BLK)
        q_here, do_here = q_ref[top, cols], do_ref[top, cols]
        both = jnp.concatenate([q_here, do_here], axis=0)
        lse = lse_ref[h, top, :]
        delta = jnp.sum(do_here.astype(F32) * top_ref[h], axis=-1, keepdims=True)
        span = max(d for d in (16, 12, 8, 2) if total % d == 0)
        step = span * BLK

        def part(i, dq):
            keys = kv_ref[h, pl.ds(i * span, span)].reshape(step, pair)
            s_dp = dot_nt(both, keys)
            token = i * step + lax.broadcasted_iota(jnp.int32, (1, step), 1)
            p = jnp.exp(s_dp[: 2 * BLK] + jnp.where(token < length, 0.0, NEG) - lse)
            ds = (p * (s_dp[2 * BLK :] - delta)).astype(BF16)
            d_keys = dot_tn(jnp.concatenate([ds, p.astype(BF16)], axis=0), both)
            acc[pl.ds(1 + i * span, span)] += d_keys.reshape(span, BLK, pair)
            return dq + dot(ds, keys)

        dq = lax.fori_loop(0, total // span, part, jnp.zeros((2 * BLK, pair), F32))
        joined[top, cols] = dq.astype(BF16)

    sums[0] = jnp.zeros((BLK, pair), F32)

    def prefix(k, carry):
        carry = carry + rand[perm_ref[layer, h, k]]
        sums[k + 1] = carry
        return carry

    lax.fori_loop(0, rows_here * 3, prefix, jnp.zeros((BLK, pair), F32))
    several = 4 if total % 4 == 0 else 1

    def settle(i, carry):
        for u in range(several):
            j = i * several + u
            low, high = start_ref[layer, h, j], start_ref[layer, h, j + 1]
            dkv[h, j] = (acc[j + 1] + (sums[high] - sums[low])).astype(BF16)
        return carry

    lax.fori_loop(0, total // several, settle, 0)


def project_back_kernel(
    count,
    heads,
    owner,
    ids_ref,
    len_ref,
    perm_ref,
    start_ref,
    q_ref,
    kv_ref,
    do_ref,
    lse_ref,
    top_ref,
    dr1_ref,
    x_any,
    w_any,
    dense_any,
    extra_ref,
    *refs,
):
    if owner == 0:
        small_ref, refs = refs[0], refs[1:]
    gw_ref, gv_ref, dx_ref, both_ref, out_ref = refs[:5]
    refs = refs[5:]
    if owner == 0:
        small_done, refs = refs[0], refs[1:]
    result_ref, all_ref, part_any, done_ref = extra_ref, out_ref, extra_ref, out_ref
    x_ref, w_ref, dense_ref, load_sems, dkv, acc, rand, sums = refs[:8]
    handed, slots, joined, send_wide, recv_wide = refs[8:13]
    sq_send, sq_recv, sq_hold, sq_send_sem, sq_recv_sem, hand_sems, ready = refs[13:20]
    me = lax.axis_index("wide")
    mine = lax.axis_index("tensor")
    section = lax.axis_index("section")
    tok, width = x_ref.shape
    own = tok // 4
    pair = 2 * HW
    wide = heads * pair
    total = dkv.shape[1]
    rows_here = tok // BLK
    right, left = {"wide": lax.rem(me + 1, count)}, {"wide": lax.rem(me + count - 1, count)}
    loads = [
        pltpu.make_async_copy(src, dst, load_sems.at[i])
        for i, (src, dst) in enumerate(
            ((dense_any, dense_ref), (w_any.at[owner], w_ref), (x_any, x_ref))
        )
    ]
    for load in loads:
        load.start()
    barrier = wide_barrier(me, count)
    for offset in (1, 2):
        pl.semaphore_signal(
            barrier, inc=1, device_id={"tensor": tensor_peer(mine, offset)}, device_id_type=MESH
        )
    greet(barrier, section, 4)
    blocks = sub_blocks(own)
    sq = Square(mine, own, width, blocks, sq_send, sq_recv, sq_hold, sq_send_sem, sq_recv_sem)
    sq.scatters = (0,)
    split = dense_ref.shape[0] // 2 if owner == 1 else dense_ref.shape[0]
    low, high = pl.ds(0, split), pl.ds(split, dense_ref.shape[0] - split)

    def hand_over(rows, to):
        return remote(
            dense_ref.at[rows], handed.at[rows], hand_sems.at[0], hand_sems.at[1], {"section": to}
        )

    if owner == 0:
        part, cross, small_up, small_cross, part_sems, small_sems = refs[20:]
        line = Line(count)

        def small_in(source):
            return remote(source, small_up, small_sems.at[0], small_sems.at[1], line.inward)

        def small_across():
            return remote(small_up, small_cross, small_sems.at[2], small_sems.at[3], line.inward)

        def small_out():
            return remote(small_done, small_done, small_sems.at[4], small_sems.at[5], line.outward)

        load_part = pltpu.make_async_copy(part_any, part, part_sems.at[0])
        load_part.start()

        def across():
            return remote(part, cross, part_sems.at[1], part_sems.at[2], line.inward)

        def outwards():
            return remote(done_ref, done_ref, part_sems.at[3], part_sems.at[4], line.outward)

        load_part.wait()

        @pl.when(line.is_middle)
        def _():
            across().start()

        @pl.when(line.no_outer)
        def _():
            small_in(small_ref).start()

    loads[0].wait()

    @pl.when(section == 1)
    def _():
        hand_over(low, 0).start()

    if owner == 1:
        tell_ready(ready, section)
        for j in range(blocks):
            all_ref[sq.rows(mine, j), :] = result_ref[j * sq.sub : (j + 1) * sq.sub, :]
            sq.share(1, j, all_ref)
    has_right, has_left = me < count - 1, me > 0

    def keys(shard):
        return pl.ds(shard * rows_here, rows_here)

    def hop(side, shard, h):
        return remote(
            slots.at[side, shard, h],
            slots.at[side, shard, h],
            send_wide.at[side, shard, h],
            recv_wide.at[side, shard, h],
            right if side == 0 else left,
        )

    def pass_on(side, shard, h, more):
        @pl.when(more)
        def _():
            hop(side, shard, h).wait_recv()
            slots[side, shard, h] = (
                slots[side, shard, h].astype(F32) + dkv[h, keys(shard)].astype(F32)
            ).astype(BF16)

        @pl.when(jnp.logical_not(more))
        def _():
            slots[side, shard, h] = dkv[h, keys(shard)]

        hop(side, shard, h).start()

    def step(h, k):
        shard_r, shard_l = count - 1 - k, k

        def rightwards():
            @pl.when(shard_r > me)
            def _():
                pass_on(0, shard_r, h, has_left)

        def leftwards():
            @pl.when(shard_l < me)
            def _():
                pass_on(1, shard_l, h, has_right)

        @pl.when(me < count // 2)
        def _():
            rightwards()
            leftwards()

        @pl.when(me >= count // 2)
        def _():
            leftwards()
            rightwards()

    def steps(h, first):
        def one(k, carry):
            step(h, k)
            return carry

        lax.fori_loop(first, count - 1, one, 0)

    groups = rows_here // grouping(rows_here)
    state = (q_ref, kv_ref, do_ref, lse_ref, top_ref, joined, dkv, acc, rand, sums)
    for h in range(heads):

        def hook(g):
            if h > 0:

                @pl.when(g < count - 1)
                def _():
                    step(h - 1, g)

        attend_back(h, owner, total, (ids_ref, len_ref, perm_ref, start_ref), state, hook)
        if h > 0:
            steps(h - 1, groups)
        if owner == 0 and h == 0:

            @pl.when(line.has_outer)
            def _():
                small_in(small_ref).wait_recv()
                small_up[...] = (
                    small_up[...].astype(F32) + small_ref[...].astype(F32)
                ).astype(BF16)

            @pl.when(line.has_outer & line.is_middle)
            def _():
                small_across().start()

            @pl.when(line.has_outer & line.not_middle)
            def _():
                small_in(small_up).start()

        if owner == 0 and h == heads - 2:

            @pl.when(line.is_middle)
            def _():
                small_across().wait_recv()
                small_done[...] = (
                    small_up[...].astype(F32) + small_cross[...].astype(F32)
                ).astype(BF16)
                across().wait_recv()

                def add(i, carry):
                    span = pl.ds(pl.multiple_of(i * PIECE, 16), PIECE)
                    done_ref[span, :] = (
                        part[span, :].astype(F32) + cross[span, :].astype(F32)
                    ).astype(BF16)
                    return carry

                lax.fori_loop(0, part.shape[0] // PIECE, add, 0)

            @pl.when(line.is_middle & line.has_outer)
            def _():
                small_out().start()
                outwards().start()

    if owner == 1:

        @pl.when(section == 0)
        def _():
            pl.semaphore_wait(ready, 1)
            hand_over(high, 1).start()

    steps(heads - 1, 0)
    for load in loads[1:]:
        load.wait()

    def add_up(first, last):
        def add(i, carry):
            span = pl.ds(pl.multiple_of(i * PIECE, 16), PIECE)
            both_ref[span, :] = (
                dense_ref[span, :].astype(F32) + handed[span, :].astype(F32)
            ).astype(BF16)
            return carry

        lax.fori_loop(first, last, add, 0)

    @pl.when(section == 0)
    def _():
        hand_over(low, 0).wait_recv()
        add_up(0, split // PIECE)

    if owner == 1:

        @pl.when(section == 1)
        def _():
            hand_over(high, 1).wait_recv()
            add_up(split // PIECE, dense_ref.shape[0] // PIECE)

    for h in range(heads):
        cols = slice(wide + h * pair, wide + (h + 1) * pair)

        @pl.when(has_left)
        def _():
            hop(0, me, h).wait_recv()

        @pl.when(has_right)
        def _():
            hop(1, me, h).wait_recv()

        here = dkv[h, keys(me)].astype(F32)
        from_left = jnp.where(has_left, slots[0, me, h].astype(F32), 0.0)
        from_right = jnp.where(has_right, slots[1, me, h].astype(F32), 0.0)
        joined[:, cols] = (here + from_left + from_right).astype(BF16).reshape(tok, pair)

    if owner == 1:
        for j in range(blocks):
            sq.relay_share(1, j, all_ref)

    def back(index, j):
        return dot(joined[sq.rows(index, j), :], w_ref[...])

    for j in range(blocks):
        sq.give_diagonal(0, j, back(sq.d, j))
    for j in range(blocks):
        sq.give_x(0, j, back(sq.x, j))
        sq.give_y(0, j, back(sq.y, j))
    for j in range(blocks):
        sq.relay_sum(0, j)
    for h in range(heads):
        at = h * 2 * HW
        gw_ref[h * HW : (h + 1) * HW, :] = dot_tn(joined[:, at : at + 2 * HW], x_ref[...])[
            :HW
        ].astype(BF16)
        gw_ref[heads * HW + at : heads * HW + at + 2 * HW, :] = dot_tn(
            joined[:, wide + at : wide + at + 2 * HW], x_ref[...]
        ).astype(BF16)
    gv_ref[...] = jnp.sum(joined[...].astype(F32), axis=0, keepdims=True)
    for j in range(blocks):
        rows = slice(j * sq.sub, (j + 1) * sq.sub)
        total = sq.total(0, j, back(mine, j) + dr1_ref[rows, :]).astype(BF16)
        dx_ref[rows, :] = total
    if owner == 1:
        for j in range(blocks):
            sq.have_all(1, j, all_ref)
    sq.close()

    @pl.when(section == 1)
    def _():
        hand_over(low, 0).wait_send()

    if owner == 1:

        @pl.when(section == 0)
        def _():
            hand_over(high, 1).wait_send()

    if owner == 0:

        @pl.when(line.is_middle)
        def _():
            small_across().wait_send()
            across().wait_send()

        @pl.when(line.not_middle)
        def _():
            small_in(small_ref).wait_send()
            small_out().wait_recv()
            outwards().wait_recv()

        @pl.when(line.not_middle & line.has_outer)
        def _():
            small_out().start()
            outwards().start()

        @pl.when(line.has_outer)
        def _():
            small_out().wait_send()
            outwards().wait_send()

    def drain(k, carry):
        shard_r, shard_l = count - 1 - k, k
        for h in range(heads):

            @pl.when(shard_r > me)
            def _():
                hop(0, shard_r, h).wait_send()

            @pl.when(shard_l < me)
            def _():
                hop(1, shard_l, h).wait_send()

        return carry

    lax.fori_loop(0, count - 1, drain, 0)


def project_back(
    scalars_, q, kv, do, lse, top, x, dr1, wt, gw, extra, small, layer, count, collective_id
):
    tok, width = x.shape
    heads, total, _, pair = kv.shape
    own = tok // 4
    wide = heads * pair
    rows_here = tok // BLK
    operands = [q, kv, do, lse, top, dr1]
    out = (tok, width) if layer == 1 else extra.shape
    parts = []
    if layer == 0:
        parts = [pltpu.VMEM(out, BF16)] * 2 + [pltpu.VMEM(small[0].shape, BF16)] * 2
        parts += [pltpu.SemaphoreType.DMA((5,)), pltpu.SemaphoreType.DMA((6,))]
    return pl.pallas_call(
        functools.partial(project_back_kernel, count, heads, layer),
        out_shape=[
            jax.ShapeDtypeStruct((wide + wide // 2, width), BF16),
            jax.ShapeDtypeStruct((1, 2 * wide), F32),
            jax.ShapeDtypeStruct((own, width), BF16),
            jax.ShapeDtypeStruct(gw.shape, BF16),
        ]
        + [jax.ShapeDtypeStruct(out, BF16)]
        + [jax.ShapeDtypeStruct(a.shape, BF16) for a in small],
        grid=(1,),
        in_specs=[scalars()] * 4
        + [whole(*a.shape) for a in operands]
        + [anywhere()] * 3
        + [whole(own, width) if layer == 1 else anywhere()]
        + [whole(*a.shape) for a in small],
        out_specs=[
            whole(wide + wide // 2, width),
            whole(1, 2 * wide),
            whole(own, width),
            whole(*gw.shape),
        ]
        + [whole(*out)]
        + [whole(*a.shape) for a in small],
        scratch_shapes=[
            pltpu.VMEM((tok, width), BF16),
            pltpu.VMEM((2 * wide, width), BF16),
            pltpu.VMEM(gw.shape, BF16),
            pltpu.SemaphoreType.DMA((3,)),
            pltpu.VMEM((heads, total, BLK, pair), BF16),
            pltpu.VMEM((total + 2, BLK, pair), F32),
            pltpu.VMEM((rows_here * 3, BLK, pair), F32),
            pltpu.VMEM((rows_here * 3 + 1, BLK, pair), F32),
            pltpu.VMEM(gw.shape, BF16),
            pltpu.VMEM((2, count, heads, rows_here, BLK, pair), BF16),
            pltpu.VMEM((tok, 2 * wide), BF16),
            pltpu.SemaphoreType.DMA((2, count, heads)),
            pltpu.SemaphoreType.DMA((2, count, heads)),
        ]
        + square_scratch(1, 2, own, width)
        + [pltpu.SemaphoreType.DMA((2,)), pltpu.SemaphoreType.REGULAR]
        + parts,
        compiler_params=params(collective_id),
        name="project_back",
    )(*scalars_, *operands, x, wt, gw, extra, *small)


def greet(barrier, section, expected):
    @pl.when(section == 0)
    def _():
        pl.semaphore_signal(barrier, inc=1, device_id={"section": 1}, device_id_type=MESH)

    pl.semaphore_wait(barrier, expected + section)


def tell_ready(ready, section):
    @pl.when(section == 1)
    def _():
        pl.semaphore_signal(ready, inc=1, device_id={"section": 0}, device_id_type=MESH)


def await_ready(ready, section):
    @pl.when(section == 0)
    def _():
        pl.semaphore_wait(ready, 1)


class Line:
    def __init__(self, count):
        w = lax.axis_index("wide")
        middle = count // 2
        low = w < middle
        self.inward = {"wide": jnp.where(low, w + 1, w - 1)}
        self.outward = {"wide": lax.rem(jnp.where(low, w + count - 1, w + 1), count)}
        self.has_outer = (w > 0) & (w < count - 1)
        self.no_outer = (w == 0) | (w == count - 1)
        self.is_middle = (w == middle - 1) | (w == middle)
        self.not_middle = (w < middle - 1) | (w > middle)


class Chain:
    def __init__(self, count, section, owner, sect, up, done, sems, segments):
        self.sect, self.up, self.done = sect, up, done
        self.r_sect, self.s_in, self.r_up, self.r_done, self.s_out, self.s_sect = sems
        self.segments = segments
        w = lax.axis_index("wide")
        middle = count // 2
        low = w < middle
        self.inward = {"wide": jnp.where(low, w + 1, w - 1)}
        self.outward = {"wide": lax.rem(jnp.where(low, w + count - 1, w + 1), count)}
        self.has_outer = (w > 0) & (w < count - 1)
        self.no_outer = (w == 0) | (w == count - 1)
        self.is_middle = (w == middle - 1) | (w == middle)
        self.not_middle = (w < middle - 1) | (w > middle)
        self.owner, self.mine = owner, section == owner
        self.other = {"section": 1 - section}

    def span(self, i, base):
        return pl.ds(pl.multiple_of((i - base) * PIECE, 16), PIECE)

    def size(self):
        return sum(size for _, _, _, size, _ in self.segments)

    def first(self):
        return min(start for _, _, start, _, _ in self.segments)

    def handed(self, ref, i, base):
        return remote(
            ref.at[self.span(i, base)],
            self.sect.at[i],
            self.s_sect.at[i],
            self.r_sect.at[i],
            self.other,
        )

    def to_up(self, i):
        return remote(self.sect.at[i], self.up.at[i], self.s_in.at[i], self.r_up.at[i], self.inward)

    def to_middle(self, i):
        return remote(
            self.sect.at[i], self.done.at[i], self.s_in.at[i], self.r_done.at[i], self.inward
        )

    def to_outer(self, i):
        return remote(
            self.done.at[i], self.done.at[i], self.s_out.at[i], self.r_done.at[i], self.outward
        )

    def pieces(self, lo, hi, body):
        for ref, base, start, size, shared in self.segments:
            first, last = max(lo, start), min(hi, start + size)
            if first < last:

                def step(i, carry, ref=ref, base=base, shared=shared):
                    body(i, ref, base, shared)
                    return carry

                lax.fori_loop(first, last, step, 0)

    def hand_over(self):
        @pl.when(jnp.logical_not(self.mine))
        def _():
            def step(i, ref, base, shared):
                if shared:
                    self.handed(ref, i, base).start()

            self.pieces(0, 1 << 20, step)

    def add(self, i, ref, base, shared):
        value = ref[self.span(i, base), :].astype(F32)
        if shared:
            self.handed(ref, i, base).wait_recv()
            value += self.sect[i].astype(F32)
        return value

    def send_in(self, i):
        @pl.when(self.is_middle)
        def _():
            self.to_middle(i).start()

        @pl.when(self.not_middle)
        def _():
            self.to_up(i).start()

    def give(self, i, ref, base, shared):
        self.sect[i] = self.add(i, ref, base, shared).astype(BF16)
        self.send_in(i)

    def relay(self, i, ref, base, shared):
        value = self.add(i, ref, base, shared)
        self.to_up(i).wait_recv()
        self.sect[i] = (value + self.up[i].astype(F32)).astype(BF16)
        self.send_in(i)

    def settle(self, i, ref, base, shared):
        self.to_middle(i).wait_recv()

        @pl.when(self.is_middle)
        def _():
            self.done[i] = (self.sect[i].astype(F32) + self.done[i].astype(F32)).astype(BF16)

        @pl.when(self.has_outer)
        def _():
            self.to_outer(i).start()

    def inwards(self, lo, hi):
        @pl.when(self.mine & self.no_outer)
        def _():
            self.pieces(lo, hi, self.give)

        @pl.when(self.mine & self.has_outer)
        def _():
            for i in range(lo, hi):
                self.pieces(i, i + 1, self.relay)
                self.pieces(i - LAG, i - LAG + 1, self.settle)

    def rest(self):
        end = self.first() + self.size()

        @pl.when(self.mine & self.no_outer)
        def _():
            self.pieces(0, end, self.settle)

        @pl.when(self.mine & self.has_outer)
        def _():
            self.pieces(end - LAG, end, self.settle)

    def close(self):
        @pl.when(self.mine)
        def _():
            self.pieces(0, 1 << 20, lambda i, ref, base, shared: self.to_up(i).wait_send())

        @pl.when(self.mine & self.has_outer)
        def _():
            self.pieces(0, 1 << 20, lambda i, ref, base, shared: self.to_outer(i).wait_send())

        @pl.when(jnp.logical_not(self.mine))
        def _():
            def step(i, ref, base, shared):
                if shared:
                    self.handed(ref, i, base).wait_send()

            self.pieces(0, 1 << 20, step)


def chain_scratch(pieces, width):
    return [pltpu.VMEM((pieces, PIECE, width), BF16)] * 2 + [
        pltpu.SemaphoreType.DMA((pieces,))
    ] * 6


def finish_kernel(
    count,
    gqkv_ref,
    gw_ref,
    gvq0_ref,
    gv0_ref,
    gvq1_ref,
    gv1_ref,
    result_ref,
    dx_ref,
    old_ref,
    small_ref,
    done_ref,
    vout_ref,
    far_ref,
    all_ref,
    got_ref,
    got_small,
    vec_ref,
    sect,
    up,
    c0,
    c1,
    c2,
    c3,
    c4,
    c5,
    vsect,
    vtens,
    vup,
    vpart,
    vfin_in,
    vfin,
    vs,
    vr,
    ts,
    tr,
    far_sems,
    ready,
    *square,
):
    section = lax.axis_index("section")
    w = lax.axis_index("wide")
    t = lax.axis_index("tensor")
    barrier = wide_barrier(w, count)
    for offset in (1, 2, 3):
        pl.semaphore_signal(
            barrier, inc=1, device_id={"tensor": tensor_peer(t, offset)}, device_id_type=MESH
        )
    greet(barrier, section, 5)
    tell_ready(ready, section)
    own, width = dx_ref.shape
    blocks = sub_blocks(own)
    sq = Square(t, own, width, blocks, *square)
    sq.scatters = ()
    for at, gvq, gv in ((0, gvq0_ref, gv0_ref), (8, gvq1_ref, gv1_ref)):
        vec_ref[at : at + 1, :] = gvq[...]
        vec_ref[at + 1 : at + 8, :] = gv[1:8, :]
    gw_pieces = gw_ref.shape[0] // PIECE
    qkv_pieces = gqkv_ref.shape[0] // PIECE
    total = gw_pieces + qkv_pieces
    sems = (c0, c1, c2, c3, c4, c5)
    chain = Chain(
        count,
        section,
        0,
        sect,
        up,
        done_ref,
        sems,
        [(gw_ref, 0, 0, gw_pieces, False), (gqkv_ref, gw_pieces, gw_pieces, qkv_pieces, True)],
    )
    inward, outward, other = chain.inward, chain.outward, chain.other
    mine = pl.ds(pl.multiple_of(section * 8, 8), 8)
    theirs = pl.ds(pl.multiple_of(8 - section * 8, 8), 8)

    def v_other():
        return remote(vec_ref.at[theirs], vsect, vs.at[0], vr.at[0], other)

    def v_peer(offset, slot):
        return remote(
            vtens.at[t],
            vtens.at[slot],
            ts.at[offset - 1],
            tr.at[offset - 1],
            {"tensor": tensor_peer(t, offset)},
        )

    def v_up():
        return remote(vpart, vup, vs.at[1], vr.at[1], inward)

    def v_middle():
        return remote(vpart, vfin_in, vs.at[1], vr.at[2], inward)

    def v_outer():
        return remote(vfin, vfin_in, vs.at[2], vr.at[2], outward)

    chain.hand_over()

    def far(ref):
        return remote(ref, far_ref, far_sems.at[0], far_sems.at[1], other)

    def hand_small():
        return remote(small_ref, got_small, far_sems.at[4], far_sems.at[5], other)

    def hand_done():
        return remote(
            old_ref, got_ref, far_sems.at[2], far_sems.at[3], other
        )

    for j in range(blocks):
        all_ref[sq.rows(t, j), :] = dx_ref[j * sq.sub : (j + 1) * sq.sub, :]
        sq.share(0, j, all_ref)
    for j in range(blocks):
        sq.relay_share(0, j, all_ref)
    chain.inwards(0, gw_pieces)
    await_ready(ready, section)
    v_other().start()

    @pl.when(section == 0)
    def _():
        far(result_ref).start()
        hand_small().start()
        hand_done().start()

    v_other().wait_recv()
    vtens[t] = vec_ref[mine, :] + vsect[...]
    for offset in (1, 2, 3):
        v_peer(offset, t).start()
    chain.inwards(gw_pieces, total)
    for j in range(blocks):
        sq.have_all(0, j, all_ref)

    @pl.when(section == 1)
    def _():
        far(all_ref).start()

    for offset in (1, 2, 3):
        v_peer(offset, tensor_peer(t, offset)).wait_recv()
    shared = vtens[0] + vtens[1] + vtens[2] + vtens[3]
    row = lax.broadcasted_iota(jnp.int32, shared.shape, 0)
    value = jnp.where((row == 0) | (row == 4), vtens[t], shared)

    @pl.when(chain.has_outer)
    def _():
        v_up().wait_recv()
        vpart[...] = value + vup[...]

    @pl.when(chain.no_outer)
    def _():
        vpart[...] = value

    @pl.when(chain.is_middle)
    def _():
        v_middle().start()

    @pl.when(chain.not_middle)
    def _():
        v_up().start()

    chain.rest()
    v_middle().wait_recv()

    @pl.when(chain.is_middle)
    def _():
        vfin[...] = vpart[...] + vfin_in[...]

    @pl.when(chain.not_middle)
    def _():
        vfin[...] = vfin_in[...]

    @pl.when(chain.has_outer)
    def _():
        v_outer().start()

    vout_ref[...] = vfin[...]
    chain.close()
    sq.close()
    far(all_ref).wait()

    @pl.when(section == 0)
    def _():
        hand_small().wait_send()
        hand_done().wait_send()

    @pl.when(section == 1)
    def _():
        hand_small().wait_recv()
        hand_done().wait_recv()

    v_other().wait_send()
    v_up().wait_send()
    for offset in (1, 2, 3):
        v_peer(offset, t).wait_send()

    @pl.when(chain.has_outer)
    def _():
        v_outer().wait_send()


def finish(gqkv, gw, vectors, result, dx, old, small_old, count, collective_id):
    own, width = dx.shape
    tok = own * 4
    pieces = (gqkv.shape[0] + gw.shape[0]) // PIECE
    small = pltpu.VMEM((8, width), F32)
    operands = [gqkv, gw, *vectors, result, dx, old, small_old]
    return pl.pallas_call(
        functools.partial(finish_kernel, count),
        out_shape=[
            jax.ShapeDtypeStruct((pieces, PIECE, width), BF16),
            jax.ShapeDtypeStruct((8, width), F32),
            jax.ShapeDtypeStruct((tok, width), BF16),
            jax.ShapeDtypeStruct((tok, width), BF16),
            jax.ShapeDtypeStruct(old.shape, BF16),
            jax.ShapeDtypeStruct(small_old.shape, BF16),
        ],
        grid=(1,),
        in_specs=[whole(*a.shape) for a in operands],
        out_specs=[whole(pieces, PIECE, width), whole(8, width)]
        + [whole(tok, width)] * 2
        + [whole(*old.shape), whole(*small_old.shape)],
        scratch_shapes=[pltpu.VMEM((16, width), F32)]
        + chain_scratch(pieces, width)
        + [small, pltpu.VMEM((4, 8, width), F32)]
        + [small] * 4
        + [pltpu.SemaphoreType.DMA((3,))] * 4
        + [pltpu.SemaphoreType.DMA((6,)), pltpu.SemaphoreType.REGULAR]
        + square_scratch(1, 1, own, width),
        compiler_params=params(collective_id),
        name="finish",
    )(*operands)


def unpack_kernel(
    heads,
    sums_ref,
    low_ref,
    high_ref,
    low_small,
    high_small,
    dx_ref,
    result_ref,
    far_ref,
    vec_ref,
    ends_ref,
    gq_ref,
    gbq_ref,
    gk_ref,
    gv_ref,
    gbv_ref,
    go_ref,
    gbo_ref,
    g1_ref,
    b1_ref,
    gi_ref,
    gbi_ref,
    gf_ref,
    gbf_ref,
    g2_ref,
    b2_ref,
    buf,
    sems,
):
    section = lax.axis_index("section")
    width = gi_ref.shape[1]
    narrow = heads * HW
    wide = heads * 2 * HW
    half = low_ref.shape[0]
    low, high = pl.ds(0, half), pl.ds(half, half)
    few = low_small.shape[0]
    spans = (low, high, pl.ds(2 * half, few), pl.ds(2 * half + few, few))
    targets = tuple(buf.at[span] for span in spans)
    targets += (ends_ref.at[0, 0, 0], ends_ref.at[0, 1, 0])

    def copy(i, source):
        return pltpu.make_async_copy(source, targets[i], sems.at[i])

    @pl.when(section == 0)
    def _():
        for i, source in enumerate(
            tuple(sums_ref.at[span] for span in spans) + (dx_ref, far_ref)
        ):
            copy(i, source).start()

    @pl.when(section != 0)
    def _():
        for i, source in enumerate(
            (low_ref, high_ref, low_small, high_small, far_ref, result_ref)
        ):
            copy(i, source).start()

    for i, ref in (
        (1, gbo_ref),
        (2, g1_ref),
        (3, b1_ref),
        (4, gbi_ref),
        (5, gbf_ref),
        (6, g2_ref),
        (7, b2_ref),
    ):
        ref[...] = vec_ref[i : i + 1, :]
    row = vec_ref[0:1, :]
    cuts = [(h * 2 * HW, wide + h * 2 * HW + HW) for h in range(heads)]
    gbq_ref[...] = 0.125 * jnp.concatenate([row[:, q : q + HW] for q, _ in cuts], axis=1)
    gbv_ref[...] = jnp.concatenate([row[:, v : v + HW] for _, v in cuts], axis=1)
    for i, source in enumerate((low_ref, high_ref, low_small, high_small)):
        copy(i, source).wait()

    def take(out, scale, source, size):
        value = buf[source : source + size, :].astype(F32)
        out(0, size, value if scale is None else scale * value)

    def into(ref, first=0):
        def put(at, span, value):
            ref[0, first + at : first + at + span, :] = value

        return put

    take(into(gi_ref), None, 0, width)
    take(into(gf_ref), None, width, width)
    take(into(go_ref), None, 2 * width, narrow)
    take(into(gq_ref), 0.125, 2 * width + narrow, narrow)
    for h in range(heads):
        source = 2 * width + 2 * narrow + h * 2 * HW
        take(into(gk_ref, h * HW), None, source, HW)
        take(into(gv_ref, h * HW), None, source + HW, HW)
    for i in (4, 5):
        copy(i, far_ref).wait()


def unpack(sums, low, high, low_small, high_small, dx, result, far, vec, heads):
    rows, width = sums.shape
    narrow = heads * HW
    ends = jax.ShapeDtypeStruct((1, 2, 1) + dx.shape, BF16)
    slim = jax.ShapeDtypeStruct((1, narrow, width), F32)
    full = jax.ShapeDtypeStruct((1, width, width), F32)
    line = jax.ShapeDtypeStruct((1, width), F32)
    short = jax.ShapeDtypeStruct((1, narrow), F32)
    shapes = [ends, slim, short, slim, slim, short, slim, line, line, line]
    shapes += [full, line, full, line, line, line]
    return pl.pallas_call(
        functools.partial(unpack_kernel, heads),
        out_shape=shapes,
        grid=(1,),
        in_specs=[anywhere()] * 8 + [whole(*vec.shape)],
        out_specs=[whole(*a.shape) for a in shapes],
        scratch_shapes=[pltpu.VMEM((rows, width), BF16), pltpu.SemaphoreType.DMA((6,))],
        compiler_params=params(),
        name="unpack",
    )(sums, low, high, low_small, high_small, dx, result, far, vec)


def body(
    inputs,
    target,
    pad_mask,
    loss_mask,
    rand_blocks,
    w_query,
    b_query,
    w_key,
    w_value,
    b_value,
    w_out,
    b_out,
    ln1_gain,
    ln1_bias,
    w_in,
    b_in,
    w_ffn,
    b_ffn,
    ln2_gain,
    ln2_bias,
):
    section = lax.axis_index("section")
    count = lax.axis_size("wide")
    micro, _, tok, width = inputs.shape
    total = pad_mask.shape[2] // BLK
    heads = w_query.shape[2] // HW
    wide = heads * 2 * HW

    rand = rand_blocks[0].reshape(heads, -1)
    far_rand = lax.ppermute(rand, "section", [(0, 1), (1, 0)])
    ids = jnp.where(section == 0, jnp.stack([rand, far_rand]), jnp.stack([far_rand, rand]))
    here = lax.dynamic_slice_in_dim(ids, lax.axis_index("wide") * (tok // BLK * 3), tok // BLK * 3, 2)
    slot = jnp.arange(here.shape[2], dtype=jnp.int32)
    order = here * here.shape[2] + slot
    rank = jnp.sum((order[..., None, :] < order[..., :, None]).astype(jnp.int32), axis=-1)
    perm = jnp.sum(jnp.where(rank[..., None, :] == slot[:, None], slot, 0), axis=-1)
    block = jnp.arange(total + 1, dtype=jnp.int32)
    starts = jnp.sum((here[..., None, :] < block[:, None]).astype(jnp.int32), axis=-1)
    weight = (loss_mask * pad_mask).astype(F32).reshape(micro, -1, tok // 4)
    length = jnp.sum(lax.dynamic_index_in_dim(pad_mask, section, 0), axis=(0, 1, 2))[None]
    matrices = [jnp.swapaxes(m, 1, 2)[0] for m in (w_query, w_key, w_value)]
    matrices += [w_in[0], w_ffn[0], w_out[0]]
    vectors = [b_query, b_value, b_out, ln1_gain, ln1_bias, b_in, b_ffn, ln2_gain, ln2_bias]
    x, q, kv, att, lse, top, wt, vall, win, wffn, wout = begin(
        ids, length, inputs, matrices, vectors, count, heads, 2
    )

    saved = []
    for layer in range(2):
        if layer == 1:
            q, kv, att, lse, top = project(ids, length, x, wt, vall, layer, count, heads, 3)
        mixed, active, slope, r1, r2, x_next = dense(
            att, x, wout, win, wffn, vall, layer, 4 + layer
        )
        saved.append((x, q, kv, att, lse, top, mixed, active, slope, r1, r2))
        x = x_next
    result, grad, handed, vector_grads = x, target, (), [None, None]
    for layer in (1, 0):
        x, q, kv, att, lse, top, mixed, active, slope, r1, r2 = saved[layer]
        gw, gv, do, dr1, *middle = dense_back(
            grad,
            weight,
            r2,
            r1,
            slope,
            active,
            mixed,
            att,
            wout,
            win,
            wffn,
            vall,
            layer,
            count,
            6 + layer,
            handed,
        )
        scalars_ = (ids, length, perm, starts)
        extra, small = (result, []) if layer == 1 else (middle[0], [middle[1]])
        gqkv, gvq, grad, gw_both, out, *small_done = project_back(
            scalars_, q, kv, do, lse, top, x, dr1, wt, gw, extra, small, layer, count, 8 + layer
        )
        vector_grads[layer] = [gvq, gv]
        if layer == 1:
            handed, result = (gw_both, gqkv), out

    vectors = vector_grads[0] + vector_grads[1]
    sums, vec, far, dx, low, low_small = finish(
        gqkv, gw_both, vectors, result, grad, out, small_done[0], count, 10
    )
    ends, gq, gbq, gk, gvalue, gbv, gout, *rest = unpack(
        sums.reshape(-1, width), low, out, low_small, small_done[0], dx, result, far, vec, heads
    )
    return (
        ends,
        jnp.swapaxes(gq, 1, 2),
        gbq,
        jnp.swapaxes(gk, 1, 2),
        jnp.swapaxes(gvalue, 1, 2),
        gbv,
        gout,
        *rest,
    )


def solution(mesh):
    matrix = P("section", None, "tensor")
    rowwise = P("section", "tensor", None)
    cut = P("section", "tensor")
    plain = P("section", None)
    return jax.shard_map(
        body,
        mesh=mesh,
        in_specs=(
            P(None, None, "wide", None),
            P(None, None, "wide", None),
            P(),
            P(),
            P("section", "tensor", None, None),
            matrix,
            cut,
            matrix,
            matrix,
            cut,
            rowwise,
            plain,
            plain,
            plain,
            matrix,
            cut,
            rowwise,
            plain,
            plain,
            plain,
        ),
        out_specs=(
            P("section", None, None, "wide", None),
            matrix,
            cut,
            matrix,
            matrix,
            cut,
            rowwise,
            plain,
            plain,
            plain,
            matrix,
            cut,
            rowwise,
            plain,
            plain,
            plain,
        ),
        check_vma=False,
    )
```

time: 3390 us -> 505 us (0.15)
  waiting for transfers between devices: 1610 us -> 0.01 us
  local copies, waits for them, and re-layouts: 688 us -> 2.49 us
  Pallas kernels: 0 us -> 491 us
  blocking collectives: 345 us -> 0 us
  matrix products: 334 us -> 0 us
  other arithmetic: 300 us -> 4.74 us
  starting transfers between devices: 78 us -> 0.52 us
    unnamed x39 -> x0, waiting for transfers between devices: 938 us -> none
    pallas_call x0 -> x10, Pallas kernels: none -> 491 us  [the longest x2 152 us: project_back(): pl.pallas_call(functools.partial(project_back_kernel, count, heads, layer...]
    all_gather x12 -> x0, waiting for transfers between devices: 417 us -> none  [tensor_total(): return lax.all_gather(shares, 'tensor', axis=2, tiled=True)]
    dot_general x109 -> x0, matrix products: 334 us -> none  [the longest x6 33.5 us: sparse_scores(): jnp.einsum('shbqd,shbnd->shbqn', query_block_tiles, key_block_tiles[...,...]
    psum x7 -> x0, waiting for transfers between devices: 247 us -> none  [the longest x1 129 us: body(): lax.psum(shortened(totals), 'wide')]
    all_gather x9 -> x0, blocking collectives: 192 us -> none  [joined(): gathered = jax.tree.map(lambda a: lax.all_gather(a, axis), part)]
    psum x4 -> x0, blocking collectives: 153 us -> none  [the longest x3 135 us: broadcast(): return lax.psum(block, axis)]
    reduce_sum x58 -> x4, other arithmetic: 148 us -> 3.16 us  [the longest x1 1.38 us: body(): jnp.sum(lax.dynamic_index_in_dim(pad_mask, section, 0), axis=(0, 1, 2))]
  transfers between devices with their start and end apart: 51 -> 1, of which waited for: 31 -> 0; matrix products, arithmetic and copies ran while one was open for 15% -> 1% of each run, Pallas kernels for 0% -> 0%
where the time goes in v1:
time: 505 us; the launch traced here: 499 us
  Pallas kernels  491 us (97%)
    pallas_call x2, Pallas kernels, project_back(): pl.pallas_call(functools.partial(project_back_kernel, count, heads, layer...  152 us
    pallas_call x2, Pallas kernels, dense_back(): pl.pallas_call(functools.partial(dense_back_kernel, count, bool(old)), ou...  89.2 us
    pallas_call x2, Pallas kernels, dense(): pl.pallas_call(functools.partial(dense_kernel, last, layer), out_shape=[j...  71.8 us
    pallas_call x1, Pallas kernels, finish(): pl.pallas_call(functools.partial(finish_kernel, count), out_shape=[jax.Sh...  70 us
    pallas_call x1, Pallas kernels, begin(): pl.pallas_call(functools.partial(begin_kernel, count, heads), grid=(1,),...  54 us
    pallas_call x1, Pallas kernels, project(): pl.pallas_call(functools.partial(project_kernel, count, heads, layer), gr...  46.6 us
  transfers between devices with their start and end apart: 1, of which 0 were waited for; matrix products, arithmetic and copies ran while one was open for 1% of the time, Pallas kernels for 0%

profile of v1, /device:TPU:0, one launch (start us, length us, event | category | flops | bytes accessed | tf_op | source)
XLA Modules:
  0.0 499.5 jit_solution(10560636891536358111)
XLA Ops:
  0.6 0.8 copy.43
  1.4 0.1 reshape_squeeze.3
  1.6 0.5 collective-permute-start
  2.1 0.8 copy.42
  2.9 0.1 stack_reshape_squeeze.5
  3.0 0.9 convert_reduce_fusion.2
  3.9 0.6 copy.48
  4.5 1.4 dynamic-slice_reduce_fusion
  5.9 0.0 collective-permute-done
  5.9 0.6 add_select_fusion.ids_ref
  6.5 54.0 %begin.1 = (bf16[1024,768]{1,0:T(8,128)(2,1)}, bf16[1024,384]{1,0:T(8,128)(2,1)}, bf16[3,64,64,128]{3,2,1,0:T(8,128)(2,1)}, bf16[1024,384]{1,0:T(8,128)(2,1)}, f...) custom-call(s32[2,3,192]{2,1,0:T(4,128)} %add_select_fusion.ids_ref,, ...), custom_call_target="tpu_custom_call" | custom-call | tf_op jit(solution)/shard_map/begin/pallas_call | solution.py:439
  60.6 39.7 %dense.2 = (bf16[1024,768]{1,0:T(8,128)(2,1)}, bf16[1024,768]{1,0:T(8,128)(2,1)}, bf16[1024,768]{1,0:T(8,128)(2,1)}, f32[256,768]{1,0:T(8,128)}, f32[256,768]{1,0:T(8,128)}, /*index=5*/bf16[1024,768]{1,0:T(8,128)(2,1)}) custom-call(bf16[1024,384]{1,0:T(8,128)(2,1)} %get-tuple-element.89.att_ref.refs_5_, bf16[1024,768]{1,0:T(8,128)(2,1)} %get-tuple-element.90.x_ref.x_any, ...), custom_call_target="tpu_custom_call" | custom-call | tf_op jit(solution)/shard_map/dense/pallas_call | solution.py:765
  100.3 46.6 %project.1 = (bf16[1024,384]{1,0:T(8,128)(2,1)}, bf16[3,64,64,128]{3,2,1,0:T(8,128)(2,1)}, bf16[1024,384]{1,0:T(8,128)(2,1)}, f32[3,1024,1]{2,1,0:T(8,128)}, f32[3,128,128]{2,1,0:T(8,128)}) custom-call(s32[2,3,192]{2,1,0:T(4,128)} %add_select_fusion.ids_ref, s32[1]{0:T(128)} %bitcast.1.len_ref, bf16[1024,768]{1,0:T(8,128)(2,1)} %get-tuple-element.95.x_ref.x_any, ...), custom_call_target="tpu_custom_call" | custom-call | tf_op jit(solution)/shard_map/project/pallas_call | solution.py:490
  146.9 0.0 copy-start
  146.9 32.0 %dense.3 = (bf16[1024,768]{1,0:T(8,128)(2,1)}, bf16[1024,768]{1,0:T(8,128)(2,1)}, bf16[1024,768]{1,0:T(8,128)(2,1)}, f32[256,768]{1,0:T(8,128)}, f32[256,768]{1,0:T(8,128)}, /*index=5*/bf16[256,768]{1,0:T(8,128)(2,1)}) custom-call(bf16[1024,384]{1,0:T(8,128)(2,1)} %get-tuple-element.99.att_ref.refs_5_, bf16[1024,768]{1,0:T(8,128)(2,1)} %get-tuple-element.95.x_ref.x_any, ...), custom_call_target="tpu_custom_call" | custom-call | tf_op jit(solution)/shard_map/dense/pallas_call | solution.py:765
  179.0 0.0 copy-done
  179.0 0.1 iota_add_fusion
  179.1 0.3 convert_reduce_fusion.1
  179.3 0.8 select_reduce_fusion.perm_ref
  180.1 0.7 convert_reduce_fusion.start_ref
  180.8 44.5 %dense_back.2 = (bf16[1728,768]{1,0:T(8,128)(2,1)}, f32[8,768]{1,0:T(8,128)}, bf16[1024,384]{1,0:T(8,128)(2,1)}, f32[256,768]{1,0:T(8,128)}) custom-call(bf16[2,1,1024,768]{3,2,1,0:T(8,128)(2,1)} %g_ref.1, f32[2,16,256]{2,1,0:T(8,128)} %bitcast.31, f32[256,768]{1,0:T(8,128)} %get-tuple-element.100.r2_ref, f32[256,768]{1,0:T(8,128)} %get-tuple-element.101.r1_ref, ...), custom_call_target="tpu_custom_call" | custom-call | tf_op jit(solution)/shard_map/dense_back/pallas_call | solution.py:1048
  225.4 72.2 %project_back.2 = (bf16[576,768]{1,0:T(8,128)(2,1)}, f32[1,768]{1,0:T(1,128)}, bf16[256,768]{1,0:T(8,128)(2,1)}, bf16[1728,768]{1,0:T(8,128)(2,1)}, bf16[1024,768]{1,0:T(8,128)(2,1)}) custom-call(s32[2,3,192]{2,1,0:T(4,128)} %add_select_fusion.ids_ref, s32[1]{0:T(128)} %bitcast.1.len_ref, s32[2,3,48]{2,1,0:T(4,128)} %select_reduce_fusion.perm_ref, ...), custom_call_target="tpu_custom_call" | custom-call | tf_op jit(solution)/shard_map/project_back/pallas_call | solution.py:1538
  297.5 44.7 %dense_back.3 = (bf16[1728,768]{1,0:T(8,128)(2,1)}, f32[8,768]{1,0:T(8,128)}, bf16[1024,384]{1,0:T(8,128)(2,1)}, f32[256,768]{1,0:T(8,128)}, bf16[864,768]{1,0:T(8,128)(2,1)}, /*index=5*/bf16[288,768]{1,0:T(8,128)(2,1)}) custom-call(bf16[256,768]{1,0:T(8,128)(2,1)} %get-tuple-element.111.g_ref, f32[2,16,256]{2,1,0:T(8,128)} %bitcast.32, ...), custom_call_target="tpu_custom_call" | custom-call | tf_op jit(solution)/shard_map/dense_back/pallas_call | solution.py:1048
  342.3 79.3 %project_back.3 = (bf16[576,768]{1,0:T(8,128)(2,1)}, f32[1,768]{1,0:T(1,128)}, bf16[256,768]{1,0:T(8,128)(2,1)}, bf16[1728,768]{1,0:T(8,128)(2,1)}, bf16[864,768]{1,0:T(8,128)(2,1)}, /*index=5*/bf16[288,768]{1,0:T(8,128)(2,1)}) custom-call(s32[2,3,192]{2,1,0:T(4,128)} %add_select_fusion.ids_ref, s32[1]{0:T(128)} %bitcast.1.len_ref, ...), custom_call_target="tpu_custom_call" | custom-call | tf_op jit(solution)/shard_map/project_back/pallas_call | solution.py:1538
  421.6 70.0 %finish.1 = (bf16[16,144,768]{2,1,0:T(8,128)(2,1)}, f32[8,768]{1,0:T(8,128)}, bf16[1024,768]{1,0:T(8,128)(2,1)}, bf16[1024,768]{1,0:T(8,128)(2,1)}, bf16[864,768]{1,0:T(8,128)(2,1)}, /*index=5*/bf16[288,768]{1,0:T(8,128)(2,1)}) custom-call(bf16[576,768]{1,0:T(8,128)(2,1)} %get-tuple-element.126.gqkv_ref, bf16[1728,768]{1,0:T(8,128)(2,1)} %get-tuple-element.127.gw_ref, ...), custom_call_target="tpu_custom_call" | custom-call | tf_op jit(solution)/shard_map/finish/pallas_call | solution.py:1975
  491.6 7.7 %unpack.1 = (bf16[1,2,1,1024,768]{4,3,2,1,0:T(8,128)(2,1)}, f32[1,192,768]{2,1,0:T(8,128)}, f32[1,192]{1,0:T(1,128)}, f32[1,192,768]{2,1,0:T(8,128)}, f32[1,192,...) custom-call(bf16[2304,768]{1,0:T(8,128)(2,1)} %bitcast.28, ...), custom_call_target="tpu_custom_call" | custom-call | tf_op jit(solution)/shard_map/unpack/pallas_call | solution.py:2109
Async XLA Ops:
  1.6 4.4 collective-permute-start
  146.9 32.1 %copy-start = (s32[2,3,192]{2,1,0:T(4,128)S(1)}, s32[2,3,192]{2,1,0:T(4,128)}, u32[]{:S(2)}) copy-start(s32[2,3,192]{2,1,0:T(4,128)} %add_select_fusion.ids_ref) | copy-start | bytes 13828

commit v2 on v1

--- a/solution.py
+++ b/solution.py
@@ -20,7 +20,7 @@
 NT_DIMS = (((1,), (1,)), ((), ()))
 TN_DIMS = (((0,), (0,)), ((), ()))
 ORDER = (3, 1, 2)
-PIECE = 144
+PIECE = 288
 LAG = 1
 
 

time: 505 us -> 507 us (level)
  no operation moved by 1% of the time
where the time goes in v2:
time: 507 us; the launch traced here: 502 us
  Pallas kernels  493 us (97%)
    pallas_call x2, Pallas kernels, project_back(): pl.pallas_call(functools.partial(project_back_kernel, count, heads, layer...  152 us
    pallas_call x2, Pallas kernels, dense_back(): pl.pallas_call(functools.partial(dense_back_kernel, count, bool(old)), ou...  89.2 us
    pallas_call x1, Pallas kernels, finish(): pl.pallas_call(functools.partial(finish_kernel, count), out_shape=[jax.Sh...  72 us
    pallas_call x2, Pallas kernels, dense(): pl.pallas_call(functools.partial(dense_kernel, last, layer), out_shape=[j...  71.8 us
    pallas_call x1, Pallas kernels, begin(): pl.pallas_call(functools.partial(begin_kernel, count, heads), grid=(1,),...  54 us
    pallas_call x1, Pallas kernels, project(): pl.pallas_call(functools.partial(project_kernel, count, heads, layer), gr...  46.6 us
  transfers between devices with their start and end apart: 1, of which 0 were waited for; matrix products, arithmetic and copies ran while one was open for 1% of the time, Pallas kernels for 0%

profile of v2, /device:TPU:0, one launch (start us, length us, event | category | flops | bytes accessed | tf_op | source)
XLA Modules:
  0.0 501.6 jit_solution(18029192291067146665)
XLA Ops:
  0.6 0.8 copy.43
  1.4 0.1 reshape_squeeze.3
  1.6 0.5 collective-permute-start
  2.1 0.8 copy.42
  2.9 0.1 stack_reshape_squeeze.5
  3.0 0.9 convert_reduce_fusion.2
  3.9 0.6 copy.48
  4.5 1.4 dynamic-slice_reduce_fusion
  5.9 0.0 collective-permute-done
  5.9 0.6 add_select_fusion.ids_ref
  6.5 54.0 %begin.1 = (bf16[1024,768]{1,0:T(8,128)(2,1)}, bf16[1024,384]{1,0:T(8,128)(2,1)}, bf16[3,64,64,128]{3,2,1,0:T(8,128)(2,1)}, bf16[1024,384]{1,0:T(8,128)(2,1)}, f...) custom-call(s32[2,3,192]{2,1,0:T(4,128)} %add_select_fusion.ids_ref,, ...), custom_call_target="tpu_custom_call" | custom-call | tf_op jit(solution)/shard_map/begin/pallas_call | solution.py:439
  60.6 39.7 %dense.2 = (bf16[1024,768]{1,0:T(8,128)(2,1)}, bf16[1024,768]{1,0:T(8,128)(2,1)}, bf16[1024,768]{1,0:T(8,128)(2,1)}, f32[256,768]{1,0:T(8,128)}, f32[256,768]{1,0:T(8,128)}, /*index=5*/bf16[1024,768]{1,0:T(8,128)(2,1)}) custom-call(bf16[1024,384]{1,0:T(8,128)(2,1)} %get-tuple-element.89.att_ref.refs_5_, bf16[1024,768]{1,0:T(8,128)(2,1)} %get-tuple-element.90.x_ref.x_any, ...), custom_call_target="tpu_custom_call" | custom-call | tf_op jit(solution)/shard_map/dense/pallas_call | solution.py:765
  100.3 46.6 %project.1 = (bf16[1024,384]{1,0:T(8,128)(2,1)}, bf16[3,64,64,128]{3,2,1,0:T(8,128)(2,1)}, bf16[1024,384]{1,0:T(8,128)(2,1)}, f32[3,1024,1]{2,1,0:T(8,128)}, f32[3,128,128]{2,1,0:T(8,128)}) custom-call(s32[2,3,192]{2,1,0:T(4,128)} %add_select_fusion.ids_ref, s32[1]{0:T(128)} %bitcast.1.len_ref, bf16[1024,768]{1,0:T(8,128)(2,1)} %get-tuple-element.95.x_ref.x_any, ...), custom_call_target="tpu_custom_call" | custom-call | tf_op jit(solution)/shard_map/project/pallas_call | solution.py:490
  146.9 0.0 copy-start
  146.9 32.0 %dense.3 = (bf16[1024,768]{1,0:T(8,128)(2,1)}, bf16[1024,768]{1,0:T(8,128)(2,1)}, bf16[1024,768]{1,0:T(8,128)(2,1)}, f32[256,768]{1,0:T(8,128)}, f32[256,768]{1,0:T(8,128)}, /*index=5*/bf16[256,768]{1,0:T(8,128)(2,1)}) custom-call(bf16[1024,384]{1,0:T(8,128)(2,1)} %get-tuple-element.99.att_ref.refs_5_, bf16[1024,768]{1,0:T(8,128)(2,1)} %get-tuple-element.95.x_ref.x_any, ...), custom_call_target="tpu_custom_call" | custom-call | tf_op jit(solution)/shard_map/dense/pallas_call | solution.py:765
  179.0 0.0 copy-done
  179.0 0.1 iota_add_fusion
  179.1 0.3 convert_reduce_fusion.1
  179.3 0.8 select_reduce_fusion.perm_ref
  180.1 0.7 convert_reduce_fusion.start_ref
  180.8 44.5 %dense_back.2 = (bf16[1728,768]{1,0:T(8,128)(2,1)}, f32[8,768]{1,0:T(8,128)}, bf16[1024,384]{1,0:T(8,128)(2,1)}, f32[256,768]{1,0:T(8,128)}) custom-call(bf16[2,1,1024,768]{3,2,1,0:T(8,128)(2,1)} %g_ref.1, f32[2,16,256]{2,1,0:T(8,128)} %bitcast.31, f32[256,768]{1,0:T(8,128)} %get-tuple-element.100.r2_ref, f32[256,768]{1,0:T(8,128)} %get-tuple-element.101.r1_ref, ...), custom_call_target="tpu_custom_call" | custom-call | tf_op jit(solution)/shard_map/dense_back/pallas_call | solution.py:1048
  225.4 72.2 %project_back.2 = (bf16[576,768]{1,0:T(8,128)(2,1)}, f32[1,768]{1,0:T(1,128)}, bf16[256,768]{1,0:T(8,128)(2,1)}, bf16[1728,768]{1,0:T(8,128)(2,1)}, bf16[1024,768]{1,0:T(8,128)(2,1)}) custom-call(s32[2,3,192]{2,1,0:T(4,128)} %add_select_fusion.ids_ref, s32[1]{0:T(128)} %bitcast.1.len_ref, s32[2,3,48]{2,1,0:T(4,128)} %select_reduce_fusion.perm_ref, ...), custom_call_target="tpu_custom_call" | custom-call | tf_op jit(solution)/shard_map/project_back/pallas_call | solution.py:1538
  297.5 44.7 %dense_back.3 = (bf16[1728,768]{1,0:T(8,128)(2,1)}, f32[8,768]{1,0:T(8,128)}, bf16[1024,384]{1,0:T(8,128)(2,1)}, f32[256,768]{1,0:T(8,128)}, bf16[864,768]{1,0:T(8,128)(2,1)}, /*index=5*/bf16[288,768]{1,0:T(8,128)(2,1)}) custom-call(bf16[256,768]{1,0:T(8,128)(2,1)} %get-tuple-element.111.g_ref, f32[2,16,256]{2,1,0:T(8,128)} %bitcast.32, ...), custom_call_target="tpu_custom_call" | custom-call | tf_op jit(solution)/shard_map/dense_back/pallas_call | solution.py:1048
  342.3 79.4 %project_back.3 = (bf16[576,768]{1,0:T(8,128)(2,1)}, f32[1,768]{1,0:T(1,128)}, bf16[256,768]{1,0:T(8,128)(2,1)}, bf16[1728,768]{1,0:T(8,128)(2,1)}, bf16[864,768]{1,0:T(8,128)(2,1)}, /*index=5*/bf16[288,768]{1,0:T(8,128)(2,1)}) custom-call(s32[2,3,192]{2,1,0:T(4,128)} %add_select_fusion.ids_ref, s32[1]{0:T(128)} %bitcast.1.len_ref, ...), custom_call_target="tpu_custom_call" | custom-call | tf_op jit(solution)/shard_map/project_back/pallas_call | solution.py:1538
  421.6 72.0 %finish.1 = (bf16[8,288,768]{2,1,0:T(8,128)(2,1)}, f32[8,768]{1,0:T(8,128)}, bf16[1024,768]{1,0:T(8,128)(2,1)}, bf16[1024,768]{1,0:T(8,128)(2,1)}, bf16[864,768]{1,0:T(8,128)(2,1)}, /*index=5*/bf16[288,768]{1,0:T(8,128)(2,1)}) custom-call(bf16[576,768]{1,0:T(8,128)(2,1)} %get-tuple-element.126.gqkv_ref, bf16[1728,768]{1,0:T(8,128)(2,1)} %get-tuple-element.127.gw_ref, ...), custom_call_target="tpu_custom_call" | custom-call | tf_op jit(solution)/shard_map/finish/pallas_call | solution.py:1975
  493.6 7.7 %unpack.1 = (bf16[1,2,1,1024,768]{4,3,2,1,0:T(8,128)(2,1)}, f32[1,192,768]{2,1,0:T(8,128)}, f32[1,192]{1,0:T(1,128)}, f32[1,192,768]{2,1,0:T(8,128)}, f32[1,192,...) custom-call(bf16[2304,768]{1,0:T(8,128)(2,1)} %bitcast.28, ...), custom_call_target="tpu_custom_call" | custom-call | tf_op jit(solution)/shard_map/unpack/pallas_call | solution.py:2109
Async XLA Ops:
  1.6 4.4 collective-permute-start
  146.9 32.1 %copy-start = (s32[2,3,192]{2,1,0:T(4,128)S(1)}, s32[2,3,192]{2,1,0:T(4,128)}, u32[]{:S(2)}) copy-start(s32[2,3,192]{2,1,0:T(4,128)} %add_select_fusion.ids_ref) | copy-start | bytes 13828

commit v3 on v1

--- a/solution.py
+++ b/solution.py
@@ -21,7 +21,7 @@
 TN_DIMS = (((0,), (0,)), ((), ()))
 ORDER = (3, 1, 2)
 PIECE = 144
-LAG = 1
+LAG = 2
 
 
 def dot(a, b):

time: 505 us -> 503 us (level)
  no operation moved by 1% of the time
where the time goes in v3:
time: 503 us; the launch traced here: 497 us
  Pallas kernels  489 us (97%)
    pallas_call x2, Pallas kernels, project_back(): pl.pallas_call(functools.partial(project_back_kernel, count, heads, layer...  152 us
    pallas_call x2, Pallas kernels, dense_back(): pl.pallas_call(functools.partial(dense_back_kernel, count, bool(old)), ou...  89.2 us
    pallas_call x2, Pallas kernels, dense(): pl.pallas_call(functools.partial(dense_kernel, last, layer), out_shape=[j...  71.8 us
    pallas_call x1, Pallas kernels, finish(): pl.pallas_call(functools.partial(finish_kernel, count), out_shape=[jax.Sh...  67.8 us
    pallas_call x1, Pallas kernels, begin(): pl.pallas_call(functools.partial(begin_kernel, count, heads), grid=(1,),...  54 us
    pallas_call x1, Pallas kernels, project(): pl.pallas_call(functools.partial(project_kernel, count, heads, layer), gr...  46.6 us
  transfers between devices with their start and end apart: 1, of which 0 were waited for; matrix products, arithmetic and copies ran while one was open for 1% of the time, Pallas kernels for 0%

profile of v3, /device:TPU:0, one launch (start us, length us, event | category | flops | bytes accessed | tf_op | source)
XLA Modules:
  0.0 497.3 jit_solution(11782403947510385227)
XLA Ops:
  0.6 0.8 copy.43
  1.4 0.1 reshape_squeeze.3
  1.6 0.5 collective-permute-start
  2.1 0.8 copy.42
  2.9 0.1 stack_reshape_squeeze.5
  3.0 0.9 convert_reduce_fusion.2
  3.9 0.6 copy.48
  4.5 1.4 dynamic-slice_reduce_fusion
  5.9 0.0 collective-permute-done
  5.9 0.6 add_select_fusion.ids_ref
  6.5 54.0 %begin.1 = (bf16[1024,768]{1,0:T(8,128)(2,1)}, bf16[1024,384]{1,0:T(8,128)(2,1)}, bf16[3,64,64,128]{3,2,1,0:T(8,128)(2,1)}, bf16[1024,384]{1,0:T(8,128)(2,1)}, f...) custom-call(s32[2,3,192]{2,1,0:T(4,128)} %add_select_fusion.ids_ref,, ...), custom_call_target="tpu_custom_call" | custom-call | tf_op jit(solution)/shard_map/begin/pallas_call | solution.py:439
  60.6 39.7 %dense.2 = (bf16[1024,768]{1,0:T(8,128)(2,1)}, bf16[1024,768]{1,0:T(8,128)(2,1)}, bf16[1024,768]{1,0:T(8,128)(2,1)}, f32[256,768]{1,0:T(8,128)}, f32[256,768]{1,0:T(8,128)}, /*index=5*/bf16[1024,768]{1,0:T(8,128)(2,1)}) custom-call(bf16[1024,384]{1,0:T(8,128)(2,1)} %get-tuple-element.89.att_ref.refs_5_, bf16[1024,768]{1,0:T(8,128)(2,1)} %get-tuple-element.90.x_ref.x_any, ...), custom_call_target="tpu_custom_call" | custom-call | tf_op jit(solution)/shard_map/dense/pallas_call | solution.py:765
  100.3 46.6 %project.1 = (bf16[1024,384]{1,0:T(8,128)(2,1)}, bf16[3,64,64,128]{3,2,1,0:T(8,128)(2,1)}, bf16[1024,384]{1,0:T(8,128)(2,1)}, f32[3,1024,1]{2,1,0:T(8,128)}, f32[3,128,128]{2,1,0:T(8,128)}) custom-call(s32[2,3,192]{2,1,0:T(4,128)} %add_select_fusion.ids_ref, s32[1]{0:T(128)} %bitcast.1.len_ref, bf16[1024,768]{1,0:T(8,128)(2,1)} %get-tuple-element.95.x_ref.x_any, ...), custom_call_target="tpu_custom_call" | custom-call | tf_op jit(solution)/shard_map/project/pallas_call | solution.py:490
  146.9 0.0 copy-start
  146.9 32.0 %dense.3 = (bf16[1024,768]{1,0:T(8,128)(2,1)}, bf16[1024,768]{1,0:T(8,128)(2,1)}, bf16[1024,768]{1,0:T(8,128)(2,1)}, f32[256,768]{1,0:T(8,128)}, f32[256,768]{1,0:T(8,128)}, /*index=5*/bf16[256,768]{1,0:T(8,128)(2,1)}) custom-call(bf16[1024,384]{1,0:T(8,128)(2,1)} %get-tuple-element.99.att_ref.refs_5_, bf16[1024,768]{1,0:T(8,128)(2,1)} %get-tuple-element.95.x_ref.x_any, ...), custom_call_target="tpu_custom_call" | custom-call | tf_op jit(solution)/shard_map/dense/pallas_call | solution.py:765
  179.0 0.0 copy-done
  179.0 0.1 iota_add_fusion
  179.1 0.3 convert_reduce_fusion.1
  179.3 0.8 select_reduce_fusion.perm_ref
  180.1 0.7 convert_reduce_fusion.start_ref
  180.8 44.5 %dense_back.2 = (bf16[1728,768]{1,0:T(8,128)(2,1)}, f32[8,768]{1,0:T(8,128)}, bf16[1024,384]{1,0:T(8,128)(2,1)}, f32[256,768]{1,0:T(8,128)}) custom-call(bf16[2,1,1024,768]{3,2,1,0:T(8,128)(2,1)} %g_ref.1, f32[2,16,256]{2,1,0:T(8,128)} %bitcast.31, f32[256,768]{1,0:T(8,128)} %get-tuple-element.100.r2_ref, f32[256,768]{1,0:T(8,128)} %get-tuple-element.101.r1_ref, ...), custom_call_target="tpu_custom_call" | custom-call | tf_op jit(solution)/shard_map/dense_back/pallas_call | solution.py:1048
  225.4 72.2 %project_back.2 = (bf16[576,768]{1,0:T(8,128)(2,1)}, f32[1,768]{1,0:T(1,128)}, bf16[256,768]{1,0:T(8,128)(2,1)}, bf16[1728,768]{1,0:T(8,128)(2,1)}, bf16[1024,768]{1,0:T(8,128)(2,1)}) custom-call(s32[2,3,192]{2,1,0:T(4,128)} %add_select_fusion.ids_ref, s32[1]{0:T(128)} %bitcast.1.len_ref, s32[2,3,48]{2,1,0:T(4,128)} %select_reduce_fusion.perm_ref, ...), custom_call_target="tpu_custom_call" | custom-call | tf_op jit(solution)/shard_map/project_back/pallas_call | solution.py:1538
  297.5 44.7 %dense_back.3 = (bf16[1728,768]{1,0:T(8,128)(2,1)}, f32[8,768]{1,0:T(8,128)}, bf16[1024,384]{1,0:T(8,128)(2,1)}, f32[256,768]{1,0:T(8,128)}, bf16[864,768]{1,0:T(8,128)(2,1)}, /*index=5*/bf16[288,768]{1,0:T(8,128)(2,1)}) custom-call(bf16[256,768]{1,0:T(8,128)(2,1)} %get-tuple-element.111.g_ref, f32[2,16,256]{2,1,0:T(8,128)} %bitcast.32, ...), custom_call_target="tpu_custom_call" | custom-call | tf_op jit(solution)/shard_map/dense_back/pallas_call | solution.py:1048
  342.3 79.3 %project_back.3 = (bf16[576,768]{1,0:T(8,128)(2,1)}, f32[1,768]{1,0:T(1,128)}, bf16[256,768]{1,0:T(8,128)(2,1)}, bf16[1728,768]{1,0:T(8,128)(2,1)}, bf16[864,768]{1,0:T(8,128)(2,1)}, /*index=5*/bf16[288,768]{1,0:T(8,128)(2,1)}) custom-call(s32[2,3,192]{2,1,0:T(4,128)} %add_select_fusion.ids_ref, s32[1]{0:T(128)} %bitcast.1.len_ref, ...), custom_call_target="tpu_custom_call" | custom-call | tf_op jit(solution)/shard_map/project_back/pallas_call | solution.py:1538
  421.6 67.8 %finish.1 = (bf16[16,144,768]{2,1,0:T(8,128)(2,1)}, f32[8,768]{1,0:T(8,128)}, bf16[1024,768]{1,0:T(8,128)(2,1)}, bf16[1024,768]{1,0:T(8,128)(2,1)}, bf16[864,768]{1,0:T(8,128)(2,1)}, /*index=5*/bf16[288,768]{1,0:T(8,128)(2,1)}) custom-call(bf16[576,768]{1,0:T(8,128)(2,1)} %get-tuple-element.126.gqkv_ref, bf16[1728,768]{1,0:T(8,128)(2,1)} %get-tuple-element.127.gw_ref, ...), custom_call_target="tpu_custom_call" | custom-call | tf_op jit(solution)/shard_map/finish/pallas_call | solution.py:1975
  489.4 7.7 %unpack.1 = (bf16[1,2,1,1024,768]{4,3,2,1,0:T(8,128)(2,1)}, f32[1,192,768]{2,1,0:T(8,128)}, f32[1,192]{1,0:T(1,128)}, f32[1,192,768]{2,1,0:T(8,128)}, f32[1,192,...) custom-call(bf16[2304,768]{1,0:T(8,128)(2,1)} %bitcast.28, ...), custom_call_target="tpu_custom_call" | custom-call | tf_op jit(solution)/shard_map/unpack/pallas_call | solution.py:2109
Async XLA Ops:
  1.6 4.4 collective-permute-start
  146.9 32.1 %copy-start = (s32[2,3,192]{2,1,0:T(4,128)S(1)}, s32[2,3,192]{2,1,0:T(4,128)}, u32[]{:S(2)}) copy-start(s32[2,3,192]{2,1,0:T(4,128)} %add_select_fusion.ids_ref) | copy-start | bytes 13828
